TPU v7x, 256 devices: a whole 4x4x8 slice. The times are simulated.
256 devices in a mesh: region: 16 (over z, core), patch: 16 (over y, x).
Axes of the slice: x: 4, y: 4, z: 8, core: 2. Of those that a mesh axis runs over, the one named last changes fastest.
Arguments:
- coarse: float32 [70, 128, 128, 128], P(None, 'region', 'patch'), may hold values from -6 to 6
- fine_patches: bfloat16 [512, 70, 4096], P(('region', 'patch')), may hold values from -6 to 6
- new_owner: int32 [512, 1], P(('region', 'patch')), may hold values from 0 to 15, as said below
- corners: int32 [512, 3], P(('region', 'patch')), may hold values from 0 to 120
- level_tags: int32 [512], P(('region', 'patch')), may hold values from 1 to 2
- diffusivity: float32 [70], replicated, may hold values from 0.005 to 0.05
- velocity: float32 [3], replicated, may hold values from 0.05 to 0.2
- growth_weight: float32 [40, 30], replicated, may hold values from -1 to 1
- yield_weight: float32 [30, 40], replicated, may hold values from -1 to 1
Outputs:
- coarse_next: float32 [70, 128, 128, 128], P(None, 'region', 'patch')
- fine_next: bfloat16 [1024, 70, 4096], P(('region', 'patch'))
Inputs may be any that keep to these rules, and one draw needn't show every extreme that they name: `new_owner`: in each region two owners receive exactly 4 patches, two receive none and the others 2; each device sends both of its patches to one owner.
All inputs are finite; a program needn't handle non-finite values.
Results may differ from a plain program's by a relative error of at most 0.001.
Values may be sent and summed in bfloat16 or wider, within the bound.
A program may use at most 192 MiB of HBM per device.

v0:
```python
import jax
import jax.numpy as jnp
from jax import lax
from jax.sharding import PartitionSpec as P

B = 16


HIGH = lax.Precision.HIGHEST


def with_halo(x, sides, width):
    for axis, dim in sides:
        size, length = (lax.axis_size(axis), x.shape[dim])
        up = [(i, (i + 1) % size) for i in range(size - 1)]
        down = [(j, i) for i, j in up]
        last = lax.slice_in_dim(x, length - width, length, axis=dim)
        leading = lax.slice_in_dim(x, 0, width, axis=dim)
        before = lax.ppermute(last, axis, up)
        after = lax.ppermute(leading, axis, down)
        x = jnp.concatenate([before, x, after], axis=dim)
    return x


def growth(state, growth_weight, yield_weight):
    sections = growth_weight.shape[0]
    soot_part = state[:sections]
    species = state[sections:]
    growth_rate = jax.nn.sigmoid(
        jnp.dot(growth_weight, species, precision=HIGH, preferred_element_type=jnp.float32)
    )
    section_flux = growth_rate * soot_part
    previous = jnp.concatenate([jnp.zeros_like(section_flux[:1]), section_flux[:-1]], axis=0)
    soot_next = soot_part + 0.5 * (previous - section_flux)
    species_next = species + 0.5 * jnp.dot(
        yield_weight, section_flux, precision=HIGH, preferred_element_type=jnp.float32
    )
    return jnp.concatenate([soot_next, species_next], axis=0)


def combine_terms(
    centre, lower_z, upper_z, lower_x, upper_x, lower_y, upper_y, params, inv_spacing
):
    diffusivity, velocity, growth_weight, yield_weight = params
    neighbours = lower_z + upper_z + lower_x + upper_x + lower_y + upper_y
    laplace = neighbours - 6.0 * centre
    upwind = (
        velocity[0] * (centre - lower_z)
        + velocity[1] * (centre - lower_x)
        + velocity[2] * (centre - lower_y)
    )
    extra = (1,) * (centre.ndim - 1)
    return (
        centre
        + diffusivity.reshape((-1,) + extra) * (inv_spacing * inv_spacing) * laplace
        - inv_spacing * upwind
    )


def transport_coarse(field, params, inv_spacing):
    growth_weight, yield_weight = (params[2], params[3])
    centre = field[:, 1:-1, 1:-1, :]
    zero_col = jnp.zeros_like(centre[..., :1])
    lower_y = jnp.concatenate([zero_col, centre[..., :-1]], axis=-1)
    upper_y = jnp.concatenate([centre[..., 1:], zero_col], axis=-1)
    moved = combine_terms(
        centre,
        field[:, :-2, 1:-1, :],
        field[:, 2:, 1:-1, :],
        field[:, 1:-1, :-2, :],
        field[:, 1:-1, 2:, :],
        lower_y,
        upper_y,
        params,
        inv_spacing,
    )
    shape = moved.shape
    return growth(moved.reshape(shape[0], -1), growth_weight, yield_weight).reshape(shape)


def transport_flat(field, params, inv_spacing, edge):
    growth_weight, yield_weight = (params[2], params[3])
    plane = edge * edge
    moved = combine_terms(
        field,
        jnp.roll(field, plane, axis=1),
        jnp.roll(field, -plane, axis=1),
        jnp.roll(field, edge, axis=1),
        jnp.roll(field, -edge, axis=1),
        jnp.roll(field, 1, axis=1),
        jnp.roll(field, -1, axis=1),
        params,
        inv_spacing,
    )
    return growth(moved, growth_weight, yield_weight)


def interp_matrix(width):
    length = 2 * width - 4
    fine_index = jnp.arange(length)
    parent = fine_index // 2 + 1
    other_parent = parent + jnp.where(fine_index % 2 == 0, -1, 1)
    columns = jnp.arange(width)
    return (
        0.75 * (columns[None, :] == parent[:, None])
        + 0.25 * (columns[None, :] == other_parent[:, None])
    ).astype(jnp.float32)


def assemble(window, patch_cells):
    matrix = interp_matrix(window.shape[-1])
    result = jnp.einsum("fabc,ia->fibc", window, matrix, precision=HIGH)
    result = jnp.einsum("fibc,jb->fijc", result, matrix, precision=HIGH)
    result = jnp.einsum("fijc,kc->fijk", result, matrix, precision=HIGH)
    edge = result.shape[-1] - 4
    interior = patch_cells.astype(jnp.float32).reshape(result.shape[0], edge, edge, edge)
    return result.at[:, 2:-2, 2:-2, 2:-2].set(interior)


def shards(
    coarse,
    fine_patches,
    new_owner,
    corners,
    level_tags,
    diffusivity,
    velocity,
    growth_weight,
    yield_weight,
):
    params = (diffusivity, velocity, growth_weight, yield_weight)
    haloed = with_halo(coarse, (("region", 1), ("patch", 2)), 2)
    coarse_next = transport_coarse(haloed[:, 1:-1, 1:-1, :], params, 0.5)
    padded = jnp.pad(haloed, ((0, 0), (0, 0), (0, 0), (2, 2)))
    count = fine_patches.shape[0]
    fields = fine_patches.shape[1]
    width = B // 2 + 4
    edge = B + 4
    receive_slots = 2 * count

    def one_patch(inputs):
        start, cells, level = inputs
        window = lax.dynamic_slice(
            padded, (0, start[0], start[1], start[2]), (fields, width, width, width)
        )
        box = assemble(window, cells).reshape(fields, -1)
        first = transport_flat(box, params, 1.0, edge)
        second = transport_flat(first, params, 1.0, edge)
        chosen = jnp.where(level == 2, second, first)
        inner = chosen.reshape(fields, edge, edge, edge)[:, 2:-2, 2:-2, 2:-2]
        return inner.reshape(fields, -1).astype(jnp.bfloat16)

    results = lax.map(one_patch, (corners, fine_patches, level_tags))
    peers = lax.axis_size("patch")
    capacity = 2
    owner = new_owner[:, 0]
    same = owner[:, None] == owner[None, :]
    earlier = jnp.arange(count)[None, :] < jnp.arange(count)[:, None]
    ranks = jnp.sum(jnp.logical_and(same, earlier), axis=1)
    slot_id = owner * capacity + ranks
    match = slot_id[None, :] == jnp.arange(peers * capacity)[:, None]
    source = jnp.sum(jnp.where(match, jnp.arange(count)[None, :], 0), axis=1)
    filled = jnp.any(match, axis=1)

    def dispatch(payload):
        taken = jnp.take(payload, source, axis=0)
        keep = filled.reshape((-1,) + (1,) * (payload.ndim - 1))
        placed = jnp.where(keep, taken, jnp.zeros_like(taken))
        return placed.reshape((peers, capacity) + payload.shape[1:])

    markers = jnp.ones((count,), jnp.bfloat16)
    received, flags = (
        lax.all_to_all(dispatch(results), "patch", split_axis=0, concat_axis=0, tiled=True),
        lax.all_to_all(dispatch(markers), "patch", split_axis=0, concat_axis=0, tiled=True),
    )
    received = received.reshape(peers * capacity, fields, -1)
    present = flags.reshape(-1) > 0
    position = jnp.cumsum(present.astype(jnp.int32)) - 1
    pick = jnp.logical_and(
        present[None, :], position[None, :] == jnp.arange(receive_slots)[:, None]
    )
    anchor = jnp.sum(jnp.where(pick, jnp.arange(peers * capacity)[None, :], 0), axis=1)
    valid = jnp.any(pick, axis=1)
    gathered = jnp.take(received, anchor, axis=0)
    fine_next = jnp.where(valid[:, None, None], gathered, jnp.zeros_like(gathered))
    return (coarse_next, fine_next)


def solution(mesh):
    placed = (
        P(None, "region", "patch", None),
        P(("region", "patch"), None, None),
        P(("region", "patch"), None),
        P(("region", "patch"), None),
        P(("region", "patch")),
        P(),
        P(),
        P(),
        P(),
    )
    return jax.shard_map(
        shards,
        mesh=mesh,
        in_specs=placed,
        out_specs=(P(None, "region", "patch", None), P(("region", "patch"), None, None)),
        check_vma=False,
    )
```

profile of v0, /device:TPU:32, one launch (start us, length us, event | category | flops | bytes accessed | tf_op | source)
XLA Modules:
  0.0 707.6 jit_solution(8821003243509898832)
XLA Ops:
  0.6 2.5 fusion.122
  3.1 1.9 collective-permute-start
  5.0 3.6 collective-permute-start.1
  10.4 3.9 collective-permute-done
  16.3 1.7 copy-done.5
  18.0 1.8 fusion.120
  19.8 3.4 collective-permute-start.2
  25.3 8.2 %all-to-all-start = ((bf16[16,1,2]{2,1,0:T(2,128)(2,1)}), bf16[16,1,2]{2,1,0:T(2,128)(2,1)}, u32[]{:S(2)}, u32[]{:S(2)}) async-start(bf16[16,1,2]{2,1,0:T(2,128)(2,1)} %copy.207), calls=%async_computation | async-start | bytes 16384 | tf_op jit(solution)/shard_map/all_to_all | solution.py:174
  34.3 3.2 copy.214
  38.7 4.0 copy.211
  42.9 3.6 collective-permute-done.3
  46.7 2.7 pad_maximum_fusion.9
  49.4 9.8 %copy.220 = f32[70,12,12,128]{0,1,3,2:T(8,128)} copy(f32[70,12,12,128]{3,0,2,1:T(8,128)} %pad_maximum_fusion.9) | data formatting | bytes 10321920
  59.3 10.7 %pad.19.clone = f32[70,12,12,132]{0,1,3,2:T(8,128)} pad(f32[70,12,12,128]{0,1,3,2:T(8,128)} %copy.220, f32[]{:T(128)} %constant.207.clone.1), padding=0_0x0_0x0_0x2_2 | pad | bytes 10483204 | tf_op jit(solution)/shard_map/jit(_pad)/pad | solution.py:134
  70.0 224.9 %while.13 = (s32[]{:T(128)}, bf16[2,70,4096]{1,2,0:T(8,128)(2,1)}, s32[2]{0:T(128)S(1)}, s32[2,3]{1,0:T(2,128)S(1)}, f32[70,12,12,132]{0,1,3,2:T(8,128)}, /*inde...) while((s32[]{:T(128)}, bf16[2,70,4096]{1,2,0:T(8,128)(2,1)}, ...), condition=%wide.region_7.8_spmd, body=%wide.region_6.7_spmd.sunk | while | flops 658525504 | bytes 165114192 | solution.py:153
  91.8 2.9 convolution_bitcast_fusion.2
  94.6 3.2 fusion.186
  97.8 5.7 fusion.187
  105.0 12.5 %scatter.6 = f32[70,20,20,20]{0,3,2,1:T(8,128)} dynamic-update-slice(f32[70,20,20,20]{0,3,2,1:T(8,128)} %fusion.187, f32[70,16,16,16]{0,3,2,1:T(8,128)S(1)} %convert.25, s32[]{:T(128)} %constant.212.clone.1..sunk, s32[]{:T(128)} %constant.199.clone.2..sunk, s32[]{:T(128)} %constant.199.clone.2..sunk, s32[]{:T(128)} %constant.199.clone.2..sunk) | dynamic-update-slice | bytes 2293764 | tf_op jit(solution)/shard_map/while/body/eval_jaxpr/scatter | solution.py:117
  117.5 5.4 reshape.348
  123.0 3.6 copy.243
  129.7 5.0 fusion.195
  140.1 5.2 fusion.204
  148.1 1.9 copy.245
  149.9 4.7 concatenate.169
  154.6 2.7 fusion.206
  157.3 5.0 concatenate.168
  162.2 5.7 copy.244
  167.9 4.9 concatenate.170
  172.9 5.7 copy.246
  178.6 1.9 copy.247
  180.5 4.8 concatenate.171
  186.4 4.5 fusion.207
  194.7 2.9 convolution_bitcast_fusion.2
  197.6 3.2 fusion.186
  200.8 5.7 fusion.187
  208.0 12.5 %scatter.6 = f32[70,20,20,20]{0,3,2,1:T(8,128)} dynamic-update-slice(f32[70,20,20,20]{0,3,2,1:T(8,128)} %fusion.187, f32[70,16,16,16]{0,3,2,1:T(8,128)S(1)} %convert.25, s32[]{:T(128)} %constant.212.clone.1..sunk, s32[]{:T(128)} %constant.199.clone.2..sunk, s32[]{:T(128)} %constant.199.clone.2..sunk, s32[]{:T(128)} %constant.199.clone.2..sunk) | dynamic-update-slice | bytes 2293764 | tf_op jit(solution)/shard_map/while/body/eval_jaxpr/scatter | solution.py:117
  220.5 5.4 reshape.348
  226.0 3.6 copy.243
  232.7 5.0 fusion.195
  243.1 5.2 fusion.204
  251.0 1.9 copy.245
  252.9 4.7 concatenate.169
  257.6 2.7 fusion.206
  260.2 5.0 concatenate.168
  265.2 5.7 copy.244
  270.9 4.9 concatenate.170
  275.8 5.7 copy.246
  281.5 1.9 copy.247
  283.5 4.8 concatenate.171
  289.4 4.5 fusion.207
  294.9 13.9 %gather_fusion = bf16[32,70,4096]{1,2,0:T(8,128)(2,1)} fusion(bf16[2,70,4096]{1,2,0:T(8,128)(2,1)} %get-tuple-element.144, s32[1024]{0:T(1024)} %pad_clamp_fusion.1), kind=kCustom, calls=%fused_computation | custom fusion | bytes 36700288 | tf_op jit(solution)/shard_map/jit(_take)/gather | solution.py:166
  308.8 36.5 %copy.215 = bf16[32,70,4096]{2,1,0:T(8,128)(2,1)} copy(bf16[32,70,4096]{1,2,0:T(8,128)(2,1)} %gather_fusion) | data formatting | bytes 36700160 | tf_op jit(solution)/shard_map/jit(_take)/gather | solution.py:166
  345.3 10.1 %select_select_fusion = bf16[16,2,70,4096]{3,2,1,0:T(8,128)(2,1)S(1)} fusion(bf16[16,2,70,4096]{3,2,1,0:T(8,128)(2,1)} %bitcast.150, pred[16,2]{1,0:T(8,128)(4,1)S(1)} %copy-done.15, pred[16,2]{1,0:T(8,128)(4,1)S(1)} %copy-done.16), kind=kLoop, calls=%fused_computation.138 | loop fusion | flops 18350080 | bytes 36700224 | tf_op jit(solution)/shard_map/jit(_where)/select_n | solution.py:168
  355.4 34.4 %copy.216 = bf16[16,2,70,4096]{3,1,2,0:T(2,128)(2,1)} copy(bf16[16,2,70,4096]{3,2,1,0:T(8,128)(2,1)S(1)} %select_select_fusion) | data formatting | bytes 36700160 | tf_op jit(solution)/shard_map/jit(_where)/select_n | solution.py:168
  389.8 9.0 %all-to-all-start.1 = ((bf16[16,2,70,4096]{3,1,2,0:T(2,128)(2,1)}), bf16[16,2,70,4096]{3,1,2,0:T(2,128)(2,1)}, u32[]{:S(2)}, u32[]{:S(2)}) async-start(bf16[16,2,70,4096]{3,1,2,0:T(2,128)(2,1)} %copy.216), calls=%async_computation.1 | async-start | bytes 36700160 | tf_op jit(solution)/shard_map/all_to_all | solution.py:173
  399.4 3.0 fusion.121
  403.7 7.2 %fusion.97 = f32[70,8,8,128]{3,2,1,0:T(8,128)S(1)} fusion(f32[70,8,8,128]{3,2,1,0:T(8,128)S(1)} %copy-done.4, f32[70,12,2,128]{3,2,1,0:T(2,128)} %copy-done.8, f32[70,12,8,128]{3,2,1,0:T(8,128)} %copy-done.5, f32[70,2,8,128]{3,2,1,0:T(8,128)} %copy-done.10, f32[70,2,8,128]{3,2,1,0:T(8,128)} %copy-done.9, f32[70,12,2,128]{3,2,1,0:T(2,128)S(1)} %copy-done.7, ...), kind=kLoop, calls=%fused_computation.159 | loop fusion | flops 13189120 | bytes 15447332 | tf_op jit(solution)/shard_map/sub | solution.py:54
  411.9 2.0 fusion.88
  416.6 1.5 slice_bitcast_fusion
  418.1 258.2 %all-to-all-done.1 = bf16[16,2,70,4096]{3,1,2,0:T(2,128)(2,1)} async-done(((bf16[16,2,70,4096]{3,1,2,0:T(2,128)(2,1)}), bf16[16,2,70,4096]{3,1,2,0:T(2,128)(2,1)}, u32[]{:S(2)}, u32[]{:S(2)}) %all-to-all-start.1) | async-done | bytes 18350112 | tf_op jit(solution)/shard_map/all_to_all | solution.py:173
  676.3 20.5 %copy.217 = bf16[16,2,70,4096]{3,2,1,0:T(8,128)(2,1)} copy(bf16[16,2,70,4096]{3,1,2,0:T(2,128)(2,1)} %all-to-all-done.1) | data formatting | bytes 36700160 | tf_op jit(solution)/shard_map/all_to_all | solution.py:173
  696.8 7.1 gather_fusion.1
  704.2 3.2 copy.218
  (139 shorter events, 43.7 us)
Async XLA Ops:
  0.6 13.8 %copy-start.3 = (f32[70,8,8,128]{3,2,1,0:T(8,128)S(1)}, f32[70,8,8,128]{3,2,1,0:T(8,128)}, u32[]{:S(2)}) copy-start(f32[70,8,8,128]{3,2,1,0:T(8,128)} %param.13) | copy-start | bytes 6881284
  3.1 11.2 %collective-permute-start = (f32[70,2,8,128]{3,2,1,0:T(8,128)}, f32[70,2,8,128]{3,2,1,0:T(8,128)S(1)}, u32[]{:S(2)}, u32[]{:S(2)}) collective-permute-start(f32[70,2,8,128]{3,2,1,0:T(8,128)} %get-tuple-element.271), channel_id=1, source_target_pairs={{0,16},{16,32},{32,48},{48,64},{64,80},{80,96},{96,112},{112,128},... | collective-permute-start | bytes 1720328 | tf_op jit(solution)/shard_map/ppermute | solution.py:19
  5.0 11.2 %collective-permute-start.1 = (f32[70,2,8,128]{3,2,1,0:T(8,128)}, f32[70,2,8,128]{3,2,1,0:T(8,128)S(1)}, u32[]{:S(2)}, u32[]{:S(2)}) collective-permute-start(f32[70,2,8,128]{3,2,1,0:T(8,128)} %get-tuple-element.270), channel_id=1, source_target_pairs={{16,0},{32,16},{48,32},{64,48},{80,64},{96,80},{112,96},{128,112},... | collective-permute-start | bytes 1720328 | tf_op jit(solution)/shard_map/ppermute | solution.py:20
  14.3 0.9 copy-start.9
  16.2 17.4 %copy-start.10 = (f32[70,2,8,128]{3,2,1,0:T(8,128)}, f32[70,2,8,128]{3,2,1,0:T(8,128)S(1)}, u32[]{:S(2)}) copy-start(f32[70,2,8,128]{3,2,1,0:T(8,128)S(1)} %collective-permute-done.1) | copy-start | bytes 1720324
  16.2 18.1 %copy-start.12 = (bf16[2,70,4096]{2,0,1:T(2,128)(2,1)S(1)}, bf16[2,70,4096]{2,0,1:T(2,128)(2,1)}, u32[]{:S(2)}) copy-start(bf16[2,70,4096]{2,0,1:T(2,128)(2,1)} %param.14) | copy-start | bytes 3440644
  16.3 1.7 copy-start.5
  19.8 22.9 %collective-permute-start.2 = (f32[70,12,2,128]{3,2,1,0:T(2,128)}, f32[70,12,2,128]{3,2,1,0:T(2,128)S(1)}, u32[]{:S(2)}, u32[]{:S(2)}) collective-permute-start(f32[70,12,2,128]{3,2,1,0:T(2,128)} %get-tuple-element.266), channel_id=1, source_target_pairs={{0,1},{1,2},{2,3},{3,4},{4,5},{5,6},{6,7},{7,8},{8,9},{9,10},{10,1... | collective-permute-start | bytes 2580488 | tf_op jit(solution)/shard_map/ppermute | solution.py:19
  23.2 23.3 %collective-permute-start.3 = (f32[70,12,2,128]{3,2,1,0:T(2,128)}, f32[70,12,2,128]{3,2,1,0:T(2,128)S(1)}, u32[]{:S(2)}, u32[]{:S(2)}) collective-permute-start(f32[70,12,2,128]{3,2,1,0:T(2,128)} %get-tuple-element.267), channel_id=1, source_target_pairs={{1,0},{2,1},{3,2},{4,3},{5,4},{6,5},{7,6},{8,7},{9,8},{10,9},{11,1... | collective-permute-start | bytes 2580488 | tf_op jit(solution)/shard_map/ppermute | solution.py:20
  25.3 364.5 %all-to-all-start = ((bf16[16,1,2]{2,1,0:T(2,128)(2,1)}), bf16[16,1,2]{2,1,0:T(2,128)(2,1)}, u32[]{:S(2)}, u32[]{:S(2)}) async-start(bf16[16,1,2]{2,1,0:T(2,128)(2,1)} %copy.207), calls=%async_computation | async-start | bytes 16384 | tf_op jit(solution)/shard_map/all_to_all | solution.py:174
  42.7 6.8 copy-start.6
  46.5 2.9 copy-start.8
  59.3 10.7 %copy-start.11 = (f32[30,40]{1,0:T(8,128)S(1)}, f32[30,40]{1,0:T(8,128)}, u32[]{:S(2)}) copy-start(f32[30,40]{1,0:T(8,128)} %param.21) | copy-start | bytes 14404
  59.3 10.7 %copy-start.13 = (f32[3]{0:T(128)S(1)}, f32[3]{0:T(128)}, u32[]{:S(2)}) copy-start(f32[3]{0:T(128)} %param.19) | copy-start | bytes 40
  59.3 10.7 %copy-start.14 = (f32[70]{0:T(128)S(1)}, f32[70]{0:T(128)}, u32[]{:S(2)}) copy-start(f32[70]{0:T(128)} %param.18) | copy-start | bytes 844
  59.3 10.7 %copy-start.17 = (f32[40,30]{0,1:T(8,128)S(1)}, f32[40,30]{0,1:T(8,128)}, u32[]{:S(2)}) copy-start(f32[40,30]{0,1:T(8,128)} %param.20) | copy-start | bytes 14404
  59.3 10.7 %copy-start.18 = (s32[2,3]{1,0:T(2,128)S(1)}, s32[2,3]{1,0:T(2,128)}, u32[]{:S(2)}) copy-start(s32[2,3]{1,0:T(2,128)} %param.16) | copy-start | bytes 76
  59.3 10.7 %copy-start.19 = (s32[2]{0:T(128)S(1)}, s32[2]{0:T(128)}, u32[]{:S(2)}) copy-start(s32[2]{0:T(128)} %param.17) | copy-start | bytes 28
  145.3 1.4 copy-start.2
  146.8 1.0 copy-start
  180.5 5.9 copy-start.1
  248.3 1.4 copy-start.2
  249.8 1.0 copy-start
  283.5 5.9 copy-start.1
  308.8 36.5 %copy-start.15 = (pred[16,2]{1,0:T(8,128)(4,1)S(1)}, pred[16,2]{1,0:T(8,128)(4,1)}, u32[]{:S(2)}) copy-start(pred[16,2]{1,0:T(8,128)(4,1)} %compare_and_fusion) | copy-start | bytes 100
  308.8 36.5 %copy-start.16 = (pred[16,2]{1,0:T(8,128)(4,1)S(1)}, pred[16,2]{1,0:T(8,128)(4,1)}, u32[]{:S(2)}) copy-start(pred[16,2]{1,0:T(8,128)(4,1)} %broadcast_in_dim.106) | copy-start | bytes 100
  389.8 9.6 %copy-start.4 = (f32[70,8,8,128]{3,2,1,0:T(8,128)S(1)}, f32[70,8,8,128]{3,2,1,0:T(8,128)}, u32[]{:S(2)}) copy-start(f32[70,8,8,128]{3,2,1,0:T(8,128)} %param.13) | copy-start | bytes 6881284
  389.8 286.5 %all-to-all-start.1 = ((bf16[16,2,70,4096]{3,1,2,0:T(2,128)(2,1)}), bf16[16,2,70,4096]{3,1,2,0:T(2,128)(2,1)}, u32[]{:S(2)}, u32[]{:S(2)}) async-start(bf16[16,2,70,4096]{3,1,2,0:T(2,128)(2,1)} %copy.216), calls=%async_computation.1 | async-start | bytes 36700160 | tf_op jit(solution)/shard_map/all_to_all | solution.py:173
  399.4 4.3 copy-start.7
where the time goes:
time: 717 us; the launch traced here: 708 us
  local copies, waits for them, and re-layouts  286 us (40%)
  waiting for transfers between devices  267 us (37%)
  other arithmetic  61.5 us (9%)
  matrix products  39.8 us (6%)
  starting transfers between devices  27.4 us (4%)
  loops' own time  24.7 us (3%)
    all_to_all x1, waiting for transfers between devices, shards(): lax.all_to_all(dispatch(results), 'patch', split_axis=0, concat_axis=0, t...  258 us
    concatenate x12, local copies, waits for them, and re-layouts, growth(): return jnp.concatenate([soot_next, species_next], axis=0)  61.5 us
    gather x2, local copies, waits for them, and re-layouts, dispatch(): taken = jnp.take(payload, source, axis=0)  50.4 us
    select_n x2, local copies, waits for them, and re-layouts, dispatch(): placed = jnp.where(keep, taken, jnp.zeros_like(taken))  35 us
    sub x5, other arithmetic, combine_terms(): centre + diffusivity.reshape((-1,) + extra) * (inv_spacing * inv_spacing)...  27.7 us
    scatter x2, local copies, waits for them, and re-layouts, assemble(): return result.at[:, 2:-2, 2:-2, 2:-2].set(interior)  25 us
    another operation x1, loops' own time, shards(): results = lax.map(one_patch, (corners, fine_patches, level_tags))  24.7 us
    all_to_all x1, local copies, waits for them, and re-layouts, shards(): lax.all_to_all(dispatch(results), 'patch', split_axis=0, concat_axis=0, t...  20.5 us
  transfers between devices with their start and end apart: 6, of which 4 were waited for; matrix products, arithmetic and copies ran while one was open for 49% of the time, Pallas kernels for 0%

commit v1 on v0

v1 whole, which is shorter than its diff:
```python
import functools

import jax
import jax.numpy as jnp
import numpy as np
from jax import lax
from jax.experimental import pallas as pl
from jax.experimental.pallas import tpu as pltpu
from jax.sharding import PartitionSpec as P

B = 16
SOOT = 40
SPEC = 30
FIELDS = 70
ROWS = 72
WIN = 12
EDGE = 20
LANES = 384
WIDE = 512
NY = 128
PLANES = 16
PEERS = 16
UNIT = 144
MESH = pl.DeviceIdType.MESH
F32 = jnp.float32
BF16 = jnp.bfloat16


def spread_matrix():
    e = np.zeros((B * B, WIDE), np.float32)
    for x in range(B):
        for y in range(B):
            e[x * B + y, (x + 2) * EDGE + y + 2] = 1.0
    return e


def interp_weights():
    m = np.zeros((EDGE, WIN), np.float32)
    for f in range(EDGE):
        parent = f // 2 + 1
        m[f, parent] = 0.75
        m[f, parent + (-1 if f % 2 == 0 else 1)] = 0.25
    v = np.zeros((256, WIDE), np.float32)
    for x in range(WIN):
        for y in range(WIN):
            v[16 * x + y, : EDGE * EDGE] = np.outer(m[:, x], m[:, y]).reshape(-1)
    return v


def dot(a, b):
    return lax.dot_general(a, b, (((1,), (0,)), ((), ())), preferred_element_type=F32)


def pack_pair(a, b):
    return jnp.concatenate([a[:64], b[:64], a[64:ROWS], b[64:ROWS]], axis=0).astype(BF16)


def unpack_pair(u):
    u = u.astype(F32)
    first = jnp.concatenate([u[:64], u[128:136]], axis=0)
    second = jnp.concatenate([u[64:128], u[136:144]], axis=0)
    return first, second


def growth(moved, gw, aw):
    soot = moved[:SOOT]
    spec = moved[SOOT:]
    sh = spec.astype(BF16)
    sl = (spec - sh.astype(F32)).astype(BF16)
    pre = dot(gw, jnp.concatenate([sh, sl, sh], axis=0))
    rate = 0.5 * jnp.tanh(0.5 * pre) + 0.5
    flux = rate * soot
    fh = flux.astype(BF16).astype(F32)
    fl = flux - fh
    return moved + dot(aw, jnp.concatenate([fh, fl, fh], axis=0).astype(BF16))


def tiled(a, n):
    return jnp.concatenate([a] * n, axis=1)


def moved_terms(c, lz, uz, lx, ux, ly, uy, own, diff, v):
    total = (lz + uz) + (lx + ux) + (ly + uy)
    return own * c + diff * total + (v[0] * lz + v[1] * lx + v[2] * ly)


def load_rows(coarse_vmem, z, x):
    return coarse_vmem[pl.ds(z * 8 + x, ROWS, stride=64), :]


def stage_coarse(coarse_hbm, coarse_vmem, sem):
    copy = pltpu.make_async_copy(coarse_hbm, coarse_vmem.at[pl.ds(0, FIELDS * 64)], sem)
    copy.start()
    coarse_vmem[FIELDS * 64 :, :] = jnp.zeros((ROWS * 64 - FIELDS * 64, NY), F32)
    return copy


def halo_kernel(coarse_hbm, got, coarse_vmem, units, in_sem, send_sem, recv_sem):
    r, p = lax.axis_index("region"), lax.axis_index("patch")
    nr, np_ = lax.axis_size("region"), lax.axis_size("patch")
    up_r, down_r = lax.rem(r + 1, nr), lax.rem(r + nr - 1, nr)
    up_p, down_p = lax.rem(p + 1, np_), lax.rem(p + np_ - 1, np_)
    sends = [
        ((up_r, p), 8, 8, 0),
        ((down_r, p), 0, 8, 8),
        ((r, up_p), 24, 8, 16),
        ((r, down_p), 16, 8, 24),
        ((up_r, up_p), 14, 2, 32),
        ((up_r, down_p), 8, 2, 34),
        ((down_r, up_p), 6, 2, 36),
        ((down_r, down_p), 0, 2, 38),
    ]
    barrier = pltpu.get_barrier_semaphore()
    for device, _, _, _ in sends:
        pl.semaphore_signal(barrier, inc=1, device_id=device, device_id_type=MESH)
    stage_coarse(coarse_hbm, coarse_vmem, in_sem).wait()

    def fill(i, _):
        units[i] = pack_pair(load_rows(coarse_vmem, 0, i), load_rows(coarse_vmem, 1, i))
        units[8 + i] = pack_pair(load_rows(coarse_vmem, 6, i), load_rows(coarse_vmem, 7, i))
        units[16 + i] = pack_pair(load_rows(coarse_vmem, i, 0), load_rows(coarse_vmem, i, 1))
        units[24 + i] = pack_pair(load_rows(coarse_vmem, i, 6), load_rows(coarse_vmem, i, 7))
        return 0

    lax.fori_loop(0, 8, fill, 0)
    pl.semaphore_wait(barrier, 8)
    copies = []
    for n, (device, src, count, dst) in enumerate(sends):
        copy = pltpu.make_async_remote_copy(
            src_ref=units.at[pl.ds(src, count)],
            dst_ref=got.at[pl.ds(dst, count)],
            send_sem=send_sem.at[n],
            recv_sem=recv_sem.at[n],
            device_id=device,
            device_id_type=MESH,
        )
        copy.start()
        copies.append(copy)
    for copy in copies:
        copy.wait()


def halo(coarse):
    return pl.pallas_call(
        halo_kernel,
        out_shape=jax.ShapeDtypeStruct((40, UNIT, NY), BF16),
        in_specs=[pl.BlockSpec(memory_space=pl.ANY)],
        out_specs=pl.BlockSpec(memory_space=pltpu.VMEM),
        scratch_shapes=[
            pltpu.VMEM((ROWS * 64, NY), F32),
            pltpu.VMEM((32, UNIT, NY), BF16),
            pltpu.SemaphoreType.DMA,
            pltpu.SemaphoreType.DMA((8,)),
            pltpu.SemaphoreType.DMA((8,)),
        ],
        compiler_params=pltpu.CompilerParams(
            collective_id=0, has_side_effects=True, vmem_limit_bytes=32 * 1024 * 1024
        ),
        name="halo",
    )(coarse)


def fill_rows(coarse_vmem, got, rows, edges):
    z_low, z_high, x_low, x_high = edges

    def own(z, _):
        for x in range(8):
            rows[z + 2, :, pl.ds((x + 2) * NY, NY)] = load_rows(coarse_vmem, z, x)
        a, b = unpack_pair(got[16 + z])
        rows[z + 2, :, pl.ds(0, NY)] = a * x_low
        rows[z + 2, :, pl.ds(NY, NY)] = b * x_low
        a, b = unpack_pair(got[24 + z])
        rows[z + 2, :, pl.ds(10 * NY, NY)] = a * x_high
        rows[z + 2, :, pl.ds(11 * NY, NY)] = b * x_high
        return 0

    lax.fori_loop(0, 8, own, 0)
    for x in range(WIN):
        if x < 2:
            low, high, side = 32 + x, 36 + x, x_low
        elif x < 10:
            low, high, side = x - 2, 8 + x - 2, 1.0
        else:
            low, high, side = 34 + x - 10, 38 + x - 10, x_high
        for unit, z, scale in ((low, 0, z_low * side), (high, 10, z_high * side)):
            a, b = unpack_pair(got[unit])
            rows[z, :, pl.ds(x * NY, NY)] = a * scale
            rows[z + 1, :, pl.ds(x * NY, NY)] = b * scale


def advance_coarse(rows, out, coef, vel, gw, aw):
    width = 4 * NY
    lane = lax.broadcasted_iota(jnp.int32, (ROWS, width), 1) % NY

    def step(i, _):
        z = i // 2 + 2
        base = pl.multiple_of((i % 2) * width, width)

        def part(dz, dx):
            return rows[z + dz, :, pl.ds(pl.multiple_of(base + (2 + dx) * NY, NY), width)]

        c = part(0, 0)
        pieces = [c[:, n * NY : (n + 1) * NY] for n in range(4)]
        ly = jnp.concatenate([pltpu.roll(t, 1, 1) for t in pieces], axis=1)
        uy = jnp.concatenate([pltpu.roll(t, NY - 1, 1) for t in pieces], axis=1)
        ly = jnp.where(lane == 0, 0.0, ly)
        uy = jnp.where(lane == NY - 1, 0.0, uy)
        moved = moved_terms(
            c, part(-1, 0), part(1, 0), part(0, -1), part(0, 1), ly, uy,
            tiled(coef[2], 4), tiled(coef[3], 4), (vel[3], vel[4], vel[5]),
        )
        new = growth(moved, gw, aw)
        for n in range(4):
            at = (z - 2) * 8 + (i % 2) * 4 + n
            out[pl.ds(at, FIELDS, stride=64), :] = new[:FIELDS, n * NY : (n + 1) * NY]
        return 0

    lax.fori_loop(0, 16, step, 0)


def build_windows(rows, corner, picks, window, weights):
    lane = lax.broadcasted_iota(jnp.int32, (NY, 256), 1)
    row = lax.broadcasted_iota(jnp.int32, (NY, 256), 0)
    start = jnp.where(lane < NY, corner[0], corner[1]) - 2
    slot = lane % NY
    for x in range(8):
        at = slot - 16 * x
        hit = jnp.logical_and(jnp.logical_and(at >= 0, at < WIN), row == start + at)
        picks[pl.ds(x * NY, NY), :] = jnp.where(hit, 1.0, 0.0).astype(BF16)
    v = weights[...]

    def group(g, _):
        z = g * 3
        lhs = rows[pl.ds(z, 3)].reshape(3 * ROWS, WIN * NY).astype(BF16)
        first = dot(lhs[:, : 8 * NY], picks[...]).astype(BF16)
        second = dot(lhs[:, 8 * NY :], picks[: 4 * NY, :]).astype(BF16)
        for n in range(2):
            cut = slice(n * NY, (n + 1) * NY)
            both = jnp.concatenate([first[:, cut], second[:, cut]], axis=1)
            window[n, pl.ds(z, 3)] = dot(both, v).reshape(3, ROWS, WIDE)
        return 0

    lax.fori_loop(0, 4, group, 0)


def build_ghosted(window, cells, ghosted, spread):
    lane = lax.broadcasted_iota(jnp.int32, (ROWS, WIDE), 1)
    x, y = lane // EDGE, lane % EDGE
    inside = (x >= 2) & (x < 18) & (y >= 2) & (y < 18)
    e = spread[...]
    pad = jnp.zeros((ROWS - FIELDS, 256), F32)

    def blend(n, f, parent, other):
        return 0.75 * window[n, parent] + 0.25 * window[n, other]

    for n in range(2):
        for f in (0, 1, 18, 19):
            parent = f // 2 + 1
            ghosted[n, f] = blend(n, f, parent, parent + (-1 if f % 2 == 0 else 1))

    def group(g, _):
        for n in range(2):
            planes = []
            for k in range(4):
                at = pl.multiple_of((g * 4 + k) * 256, 256)
                planes.append(jnp.concatenate([cells[n, :, pl.ds(at, 256)].astype(F32), pad], axis=0))
            full = dot(jnp.concatenate(planes, axis=0).astype(BF16), e)
            for k in range(4):
                f = 2 + g * 4 + k
                parent = 2 + g * 2 + k // 2
                other = parent + (-1 if k % 2 == 0 else 1)
                ghosted[n, f] = jnp.where(inside, full[k * ROWS : (k + 1) * ROWS], blend(n, f, parent, other))
        return 0

    lax.fori_loop(0, 4, group, 0)


def first_step(ghosted, z, coef, vel, gw, aw):
    moved = []
    for n in range(2):
        wide = ghosted[n, z]
        c = wide[:, :LANES]
        moved.append(
            moved_terms(
                c,
                ghosted[n, z - 1, :, :LANES],
                ghosted[n, z + 1, :, :LANES],
                pltpu.roll(c, EDGE, 1),
                pltpu.roll(wide, WIDE - EDGE, 1)[:, :LANES],
                pltpu.roll(c, 1, 1),
                pltpu.roll(c, LANES - 1, 1),
                tiled(coef[0], 3), tiled(coef[1], 3), (vel[0], vel[1], vel[2]),
            )
        )
    return growth(jnp.concatenate(moved, axis=1), gw, aw)


def second_step(once, z, coef, vel, gw, aw):
    moved = []
    for n in range(2):
        cut = pl.ds(n * LANES, LANES)
        c = once[z, :, cut]
        moved.append(
            moved_terms(
                c,
                once[z - 1, :, cut],
                once[z + 1, :, cut],
                pltpu.roll(c, EDGE, 1),
                pltpu.roll(c, LANES - EDGE, 1),
                pltpu.roll(c, 1, 1),
                pltpu.roll(c, LANES - 1, 1),
                tiled(coef[0], 3), tiled(coef[1], 3), (vel[0], vel[1], vel[2]),
            )
        )
    return growth(jnp.concatenate(moved, axis=1), gw, aw)


def advance_kernel(
    corner, level, vel, coarse_hbm, got, cells, coef, gw_ref, aw_ref, spread, gather, weights,
    coarse_out, packed, coarse_vmem, rows, picks, window, ghosted, once, sem,
):
    r, p = lax.axis_index("region"), lax.axis_index("patch")
    nr, np_ = lax.axis_size("region"), lax.axis_size("patch")
    edges = [jnp.where(hit, 0.0, 1.0) for hit in (r == 0, r == nr - 1, p == 0, p == np_ - 1)]
    stage_coarse(coarse_hbm, coarse_vmem, sem).wait()
    fill_rows(coarse_vmem, got, rows, edges)
    gw, aw = gw_ref[...], aw_ref[...]
    build_windows(rows, corner, picks, window, weights)
    build_ghosted(window, cells, ghosted, spread)
    lane = lax.broadcasted_iota(jnp.int32, (ROWS, 2 * LANES), 1)
    twice = jnp.where(lane < LANES, level[0], level[1]) == 2
    for z in (1, 2, 3):
        once[z] = first_step(ghosted, z, coef, vel, gw, aw)

    def plane(z, _):
        second = second_step(once, z, coef, vel, gw, aw)
        chosen = jnp.where(twice, second, once[z]).astype(BF16)
        ahead = jnp.minimum(z + 2, 18)
        once[ahead] = first_step(ghosted, ahead, coef, vel, gw, aw)
        pair = [dot(chosen[:, n * LANES : (n + 1) * LANES], gather[...]) for n in range(2)]
        packed[z - 2] = pack_pair(*pair)
        return 0

    lax.fori_loop(2, 18, plane, 0)
    advance_coarse(rows, coarse_out, coef, vel, gw, aw)


def advance(corner, level, vel, coarse, got, cells, coef, gw, aw):
    spread = jnp.asarray(spread_matrix(), BF16)
    gather = jnp.asarray(spread_matrix()[:, :LANES].T.copy(), BF16)
    weights = jnp.asarray(interp_weights(), BF16)
    vmem = pl.BlockSpec(memory_space=pltpu.VMEM)
    smem = pl.BlockSpec(memory_space=pltpu.SMEM)
    return pl.pallas_call(
        advance_kernel,
        out_shape=(
            jax.ShapeDtypeStruct((FIELDS * 64, NY), F32),
            jax.ShapeDtypeStruct((PLANES, UNIT, 256), BF16),
        ),
        in_specs=[smem, smem, smem, pl.BlockSpec(memory_space=pl.ANY)] + [vmem] * 8,
        out_specs=(vmem, vmem),
        scratch_shapes=[
            pltpu.VMEM((ROWS * 64, NY), F32),
            pltpu.VMEM((WIN, ROWS, WIN * NY), F32),
            pltpu.VMEM((8 * NY, 256), BF16),
            pltpu.VMEM((2, WIN, ROWS, WIDE), F32),
            pltpu.VMEM((2, EDGE, ROWS, WIDE), F32),
            pltpu.VMEM((EDGE, ROWS, 2 * LANES), F32),
            pltpu.SemaphoreType.DMA,
        ],
        compiler_params=pltpu.CompilerParams(vmem_limit_bytes=56 * 1024 * 1024),
        name="advance",
    )(corner, level, vel, coarse, got, cells, coef, gw, aw, spread, gather, weights)


def exchange_kernel(pick, keep, packed, landed, spread_in, staged, s1, r1, s2, r2):
    r, p = lax.axis_index("region"), lax.axis_index("patch")
    barrier = pltpu.get_barrier_semaphore()
    for d in range(1, PEERS):
        pl.semaphore_signal(
            barrier, inc=1, device_id=(r, lax.rem(p + d, PEERS)), device_id_type=MESH
        )
    pl.semaphore_wait(barrier, PEERS - 1)

    def first(d):
        peer = lax.rem(p + d, PEERS)
        return pltpu.make_async_remote_copy(
            src_ref=packed.at[peer],
            dst_ref=spread_in.at[p],
            send_sem=s1.at[d],
            recv_sem=r1.at[d],
            device_id=(r, peer),
            device_id_type=MESH,
        )

    def second(d):
        return pltpu.make_async_remote_copy(
            src_ref=staged.at[d],
            dst_ref=landed.at[p],
            send_sem=s2.at[d],
            recv_sem=r2.at[d],
            device_id=(r, lax.rem(p + d, PEERS)),
            device_id_type=MESH,
        )

    def each(body):
        lax.fori_loop(1, PEERS, lambda d, _: (body(d), 0)[1], 0)

    each(lambda d: first(d).start())
    spread_in[p] = packed[p]
    each(lambda d: first(d).wait())

    def item(owner, k):
        n = owner * 2 + k
        chunk = spread_in[pick[n]]
        return jnp.where(keep[n] > 0, chunk, jnp.zeros_like(chunk))

    def send(d):
        owner = lax.rem(p + d, PEERS)
        for k in range(2):
            staged[d, k] = item(owner, k)
        second(d).start()

    each(send)
    for k in range(2):
        landed[p, k] = item(p, k)
    each(lambda d: second(d).wait())


def exchange(pick, keep, packed):
    vmem = pl.BlockSpec(memory_space=pltpu.VMEM)
    smem = pl.BlockSpec(memory_space=pltpu.SMEM)
    return pl.pallas_call(
        exchange_kernel,
        out_shape=jax.ShapeDtypeStruct((PEERS, 2, UNIT, 256), BF16),
        in_specs=[smem, smem, vmem],
        out_specs=vmem,
        scratch_shapes=[
            pltpu.VMEM((PEERS, UNIT, 256), BF16),
            pltpu.VMEM((PEERS, 2, UNIT, 256), BF16),
        ]
        + [pltpu.SemaphoreType.DMA((PEERS,))] * 4,
        compiler_params=pltpu.CompilerParams(
            collective_id=1, has_side_effects=True, vmem_limit_bytes=32 * 1024 * 1024
        ),
        name="exchange",
    )(pick, keep, packed)


def place_kernel(landed, out):
    for j in range(PLANES):
        first, second = unpack_pair(landed[j, 0])
        out[0, :, pl.ds(j * 256, 256)] = first[:FIELDS].astype(BF16)
        out[1, :, pl.ds(j * 256, 256)] = second[:FIELDS].astype(BF16)


def place(landed):
    return pl.pallas_call(
        place_kernel,
        grid=(2,),
        out_shape=jax.ShapeDtypeStruct((4, FIELDS, B**3), BF16),
        in_specs=[pl.BlockSpec((PLANES, 1, UNIT, 256), lambda k: (0, k, 0, 0))],
        out_specs=pl.BlockSpec((2, FIELDS, B**3), lambda k: (k, 0, 0)),
        name="place",
    )(landed)


def split(x):
    high = lax.reduce_precision(x, 8, 7)
    return high, x - high


def parameters(diffusivity, velocity, growth_weight, yield_weight):
    flow = jnp.sum(velocity)
    d = jnp.pad(diffusivity, (0, ROWS - FIELDS))
    columns = jnp.stack([1.0 - 6.0 * d - flow, d, 1.0 - 1.5 * d - 0.5 * flow, 0.25 * d])
    coef = jnp.broadcast_to(columns[:, :, None], (4, ROWS, NY))
    vel = jnp.concatenate([velocity, 0.5 * velocity])
    gh, gl = split(jnp.pad(growth_weight, ((0, 0), (0, 32 - SPEC))))
    gw = jnp.concatenate([gh, gh, gl], axis=1).astype(BF16)
    change = jnp.eye(SOOT, k=-1, dtype=F32) - jnp.eye(SOOT, dtype=F32)
    both = 0.5 * jnp.concatenate([change, yield_weight, jnp.zeros((ROWS - FIELDS, SOOT), F32)])
    ah, al = split(both)
    aw = jnp.concatenate([ah, ah, al], axis=1).astype(BF16)
    return coef, vel, gw, aw


def shards(
    coarse, fine_patches, new_owner, corners, level_tags, diffusivity, velocity, growth_weight, yield_weight
):
    owners = lax.all_gather(new_owner[:1, 0], "patch", tiled=True)
    before = jnp.arange(PEERS)[None, :] < jnp.arange(PEERS)[:, None]
    rank = jnp.sum((owners[:, None] == owners[None, :]) & before, axis=1)
    slot = owners * 2 + rank
    match = slot[None, :] == jnp.arange(2 * PEERS)[:, None]
    pick = jnp.sum(jnp.where(match, jnp.arange(PEERS)[None, :], 0), axis=1)
    keep = jnp.any(match, axis=1).astype(jnp.int32)
    coef, vel, gw, aw = parameters(diffusivity, velocity, growth_weight, yield_weight)
    flat = coarse.reshape(FIELDS * 64, NY)
    got = halo(flat)
    coarse_next, packed = advance(corners[:, 2], level_tags, vel, flat, got, fine_patches, coef, gw, aw)
    landed = exchange(pick, keep, packed)
    return coarse_next.reshape(coarse.shape), place(landed)


def solution(mesh):
    placed = (
        P(None, "region", "patch", None),
        P(("region", "patch"), None, None),
        P(("region", "patch"), None),
        P(("region", "patch"), None),
        P(("region", "patch")),
        P(),
        P(),
        P(),
        P(),
    )
    return jax.shard_map(
        shards,
        mesh=mesh,
        in_specs=placed,
        out_specs=(P(None, "region", "patch", None), P(("region", "patch"), None, None)),
        check_vma=False,
    )
```

time: 717 us -> 148 us (0.21)
  the two profiles are of different devices: /device:TPU:32 before, /device:TPU:6 now
where the time goes in v1:
time: 148 us; the launch traced here: 145 us
  Pallas kernels  105 us (71%)
  local copies, waits for them, and re-layouts  17.3 us (12%)
  blocking collectives  14.9 us (10%)
  other arithmetic  6.46 us (4%)
    pallas_call x1, Pallas kernels, exchange(): pl.pallas_call(exchange_kernel, out_shape=jax.ShapeDtypeStruct((PEERS, 2,...  53.9 us
    pallas_call x1, Pallas kernels, advance(): pl.pallas_call(advance_kernel, out_shape=(jax.ShapeDtypeStruct((FIELDS *...  33 us
    pallas_call x1, Pallas kernels, halo(): pl.pallas_call(halo_kernel, out_shape=jax.ShapeDtypeStruct((40, UNIT, NY)...  15.7 us
    unnamed x14, local copies, waits for them, and re-layouts  15 us
    all_gather x1, blocking collectives, shards(): owners = lax.all_gather(new_owner[:1, 0], 'patch', tiled=True)  14.9 us

profile of v1, /device:TPU:6, one launch (start us, length us, event | category | flops | bytes accessed | tf_op | source)
XLA Modules:
  0.0 145.4 jit_solution(5273618229544448638)
XLA Ops:
  0.6 0.0 copy-start.1
  0.6 1.4 dynamic-slice
  2.1 1.4 slice_reduce_fusion.corner
  3.5 0.1 pad.15.clone
  3.5 1.3 bitcast_dynamic-update-slice_fusion
  4.9 14.9 %all-reduce.2 = s32[16]{0:T(128)S(1)} all-reduce(s32[16]{0:T(128)S(1)} %bitcast_dynamic-update-slice_fusion), channel_id=2, replica_groups=mesh['region'=16,'patch'=16] {'patch'}, use_global_device_ids=true, to_apply=%add.2 | all-reduce | flops 16 | bytes 128 | tf_op jit(solution)/shard_map/all_gather | solution.py:491
  19.8 0.2 convert_reduce_fusion
  20.0 0.1 fusion.2
  20.1 0.1 select_reduce_fusion.pick
  20.2 1.3 fusion.4
  22.1 1.3 pad_maximum_fusion.3.vel
  23.4 1.3 subtract_bitcast_fusion.1
  24.7 0.1 convert_subtract_fusion
  24.8 0.8 reduce-precision_convert_fusion
  25.6 0.7 pad_maximum_fusion.aw_ref
  26.3 0.8 copy.17
  27.1 0.7 pad_maximum_fusion.1.gw_ref
  27.8 0.8 broadcast_in_dim.16.coef
  28.5 2.9 %copy.18.cells = bf16[2,70,4096]{2,1,0:T(8,128)(2,1)} copy(bf16[2,70,4096]{2,0,1:T(2,128)(2,1)} %param.13) | data formatting | bytes 2293760 | tf_op args[1]
  31.4 0.0 copy-done.1
  31.4 15.7 %halo.1.got = bf16[40,144,128]{2,1,0:T(8,128)(2,1)S(1)} custom-call(f32[4480,128]{1,0:T(8,128)S(1)} %bitcast.15), custom_call_target="tpu_custom_call" | custom-call | tf_op jit(solution)/shard_map/halo/pallas_call | solution.py:144
  47.1 0.0 copy-start.2
  47.1 1.1 copy-done.2
  48.2 33.0 %advance.1 = (f32[4480,128]{1,0:T(8,128)}, bf16[16,144,256]{2,1,0:T(8,128)(2,1)}) custom-call(s32[2]{0:T(128)} %slice_reduce_fusion.corner, s32[2]{0:T(128)} %level.1, f32[6]{0:T(128)} %pad_maximum_fusion.3.vel, f32[4480,128]{1,0:T(8,128)} %bitcast.14, bf16[40,144,128]{2,1,0:T(8,128)(2,1)} %copy-done.2, bf16[2,70,4096]{2,1,0:T(8,128)(2,1)} %copy.18.cells, ...), custom_call_target="tpu_custom_call" | custom-call | tf_op jit(solution)/shard_map/advance/pallas_call | solution.py:354
  81.2 0.0 copy-start.3
  81.2 1.3 copy-done.3
  82.5 53.9 %exchange.1.landed = bf16[16,2,144,256]{3,2,1,0:T(8,128)(2,1)S(1)} custom-call(s32[32]{0:T(128)S(1)} %select_reduce_fusion.pick, s32[32]{0:T(128)S(1)} %convert_element_type.21.keep, bf16[16,144,256]{2,1,0:T(8,128)(2,1)S(1)} %copy-done.3), custom_call_target="tpu_custom_call" | custom-call | tf_op jit(solution)/shard_map/exchange/pallas_call | solution.py:433
  136.3 0.0 copy-start
  136.4 1.4 copy-done
  137.8 2.8 %place.1 = bf16[4,70,4096]{2,1,0:T(8,128)(2,1)} custom-call(bf16[16,2,144,256]{3,2,1,0:T(8,128)(2,1)} %copy-done), custom_call_target="tpu_custom_call" | custom-call | tf_op jit(solution)/shard_map/place/pallas_call | solution.py:458
  140.6 4.8 %copy.19 = bf16[4,70,4096]{2,0,1:T(4,128)(2,1)} copy(bf16[4,70,4096]{2,1,0:T(8,128)(2,1)} %place.1) | data formatting | bytes 4587520
  (7 shorter events, 0.0 us)
Async XLA Ops:
  0.6 30.8 %copy-start.1 = (f32[70,8,8,128]{3,2,1,0:T(8,128)S(1)}, f32[70,8,8,128]{3,2,1,0:T(8,128)}, u32[]{:S(2)}) copy-start(f32[70,8,8,128]{3,2,1,0:T(8,128)} %param.12) | copy-start | bytes 6881284
  47.1 1.1 copy-start.2
  81.2 1.3 copy-start.3
  136.3 1.4 copy-start

commit v2 on v1

--- a/solution.py
+++ b/solution.py
@@ -95,71 +95,6 @@
     return copy
 
 
-def halo_kernel(coarse_hbm, got, coarse_vmem, units, in_sem, send_sem, recv_sem):
-    r, p = lax.axis_index("region"), lax.axis_index("patch")
-    nr, np_ = lax.axis_size("region"), lax.axis_size("patch")
-    up_r, down_r = lax.rem(r + 1, nr), lax.rem(r + nr - 1, nr)
-    up_p, down_p = lax.rem(p + 1, np_), lax.rem(p + np_ - 1, np_)
-    sends = [
-        ((up_r, p), 8, 8, 0),
-        ((down_r, p), 0, 8, 8),
-        ((r, up_p), 24, 8, 16),
-        ((r, down_p), 16, 8, 24),
-        ((up_r, up_p), 14, 2, 32),
-        ((up_r, down_p), 8, 2, 34),
-        ((down_r, up_p), 6, 2, 36),
-        ((down_r, down_p), 0, 2, 38),
-    ]
-    barrier = pltpu.get_barrier_semaphore()
-    for device, _, _, _ in sends:
-        pl.semaphore_signal(barrier, inc=1, device_id=device, device_id_type=MESH)
-    stage_coarse(coarse_hbm, coarse_vmem, in_sem).wait()
-
-    def fill(i, _):
-        units[i] = pack_pair(load_rows(coarse_vmem, 0, i), load_rows(coarse_vmem, 1, i))
-        units[8 + i] = pack_pair(load_rows(coarse_vmem, 6, i), load_rows(coarse_vmem, 7, i))
-        units[16 + i] = pack_pair(load_rows(coarse_vmem, i, 0), load_rows(coarse_vmem, i, 1))
-        units[24 + i] = pack_pair(load_rows(coarse_vmem, i, 6), load_rows(coarse_vmem, i, 7))
-        return 0
-
-    lax.fori_loop(0, 8, fill, 0)
-    pl.semaphore_wait(barrier, 8)
-    copies = []
-    for n, (device, src, count, dst) in enumerate(sends):
-        copy = pltpu.make_async_remote_copy(
-            src_ref=units.at[pl.ds(src, count)],
-            dst_ref=got.at[pl.ds(dst, count)],
-            send_sem=send_sem.at[n],
-            recv_sem=recv_sem.at[n],
-            device_id=device,
-            device_id_type=MESH,
-        )
-        copy.start()
-        copies.append(copy)
-    for copy in copies:
-        copy.wait()
-
-
-def halo(coarse):
-    return pl.pallas_call(
-        halo_kernel,
-        out_shape=jax.ShapeDtypeStruct((40, UNIT, NY), BF16),
-        in_specs=[pl.BlockSpec(memory_space=pl.ANY)],
-        out_specs=pl.BlockSpec(memory_space=pltpu.VMEM),
-        scratch_shapes=[
-            pltpu.VMEM((ROWS * 64, NY), F32),
-            pltpu.VMEM((32, UNIT, NY), BF16),
-            pltpu.SemaphoreType.DMA,
-            pltpu.SemaphoreType.DMA((8,)),
-            pltpu.SemaphoreType.DMA((8,)),
-        ],
-        compiler_params=pltpu.CompilerParams(
-            collective_id=0, has_side_effects=True, vmem_limit_bytes=32 * 1024 * 1024
-        ),
-        name="halo",
-    )(coarse)
-
-
 def fill_rows(coarse_vmem, got, rows, edges):
     z_low, z_high, x_low, x_high = edges
 
@@ -188,7 +123,7 @@
             rows[z + 1, :, pl.ds(x * NY, NY)] = b * scale
 
 
-def advance_coarse(rows, out, coef, vel, gw, aw):
+def advance_coarse(rows, out, coef, vel, gw, aw, first):
     width = 4 * NY
     lane = lax.broadcasted_iota(jnp.int32, (ROWS, width), 1) % NY
 
@@ -215,7 +150,7 @@
             out[pl.ds(at, FIELDS, stride=64), :] = new[:FIELDS, n * NY : (n + 1) * NY]
         return 0
 
-    lax.fori_loop(0, 16, step, 0)
+    lax.fori_loop(first, first + 8, step, 0)
 
 
 def build_windows(rows, corner, picks, window, weights):
@@ -315,14 +250,111 @@
     return growth(jnp.concatenate(moved, axis=1), gw, aw)
 
 
-def advance_kernel(
-    corner, level, vel, coarse_hbm, got, cells, coef, gw_ref, aw_ref, spread, gather, weights,
-    coarse_out, packed, coarse_vmem, rows, picks, window, ghosted, once, sem,
+def remote(src, dst, send, recv, device):
+    return pltpu.make_async_remote_copy(
+        src_ref=src, dst_ref=dst, send_sem=send, recv_sem=recv, device_id=device, device_id_type=MESH
+    )
+
+
+def mod4(a):
+    return lax.rem(a + 8, 4)
+
+
+def loop(start, stop, body):
+    lax.fori_loop(start, stop, lambda i, _: (body(i), 0)[1], 0)
+
+
+def fused_kernel(
+    corner, level, vel, owner, coarse_hbm, cells, coef, gw_ref, aw_ref, spread, gather, weights,
+    coarse_out, landed,
+    coarse_vmem, rows, picks, window, ghosted, once,
+    units, got, row_tiles, tiles, order, order_smem,
+    packed, mid0, mid1, held0, held1, staged0, staged1, relay0, relay1,
+    load_sem, halo_s, halo_r, tile_s, tile_r, s1a, r1a, s1b, r1b, s2a, r2a, s2b, r2b, s3a, r3a, s3b, r3b, s4a, r4a, s4b, r4b,
 ):
     r, p = lax.axis_index("region"), lax.axis_index("patch")
     nr, np_ = lax.axis_size("region"), lax.axis_size("patch")
+    y, x = p // 4, lax.rem(p, 4)
+    up_r, down_r = lax.rem(r + 1, nr), lax.rem(r + nr - 1, nr)
+    up_p, down_p = lax.rem(p + 1, np_), lax.rem(p + np_ - 1, np_)
+    mine = mod4(y - x)
+
+    def at(yy, xx):
+        return (r, yy * 4 + xx)
+
+    halo_sends = [
+        ((up_r, p), 8, 8, 0),
+        ((down_r, p), 0, 8, 8),
+        ((r, up_p), 24, 8, 16),
+        ((r, down_p), 16, 8, 24),
+        ((up_r, up_p), 14, 2, 32),
+        ((up_r, down_p), 8, 2, 34),
+        ((down_r, up_p), 6, 2, 36),
+        ((down_r, down_p), 0, 2, 38),
+    ]
+    barrier = pltpu.get_barrier_semaphore()
+    for device, _, _, _ in halo_sends:
+        pl.semaphore_signal(barrier, inc=1, device_id=device, device_id_type=MESH)
+    for d in (1, 2, 3):
+        pl.semaphore_signal(barrier, inc=1, device_id=at(y, mod4(x + d)), device_id_type=MESH)
+        pl.semaphore_signal(barrier, inc=1, device_id=at(mod4(y + d), x), device_id_type=MESH)
+    load = stage_coarse(coarse_hbm, coarse_vmem, load_sem)
+    row_tiles[x] = jnp.full((8, NY), owner[0], jnp.int32)
+    held0[16] = jnp.zeros((UNIT, NY), BF16)
+    held1[16] = jnp.zeros((UNIT, NY), BF16)
+    load.wait()
+
+    def fill(i):
+        units[i] = pack_pair(load_rows(coarse_vmem, 0, i), load_rows(coarse_vmem, 1, i))
+        units[8 + i] = pack_pair(load_rows(coarse_vmem, 6, i), load_rows(coarse_vmem, 7, i))
+        units[16 + i] = pack_pair(load_rows(coarse_vmem, i, 0), load_rows(coarse_vmem, i, 1))
+        units[24 + i] = pack_pair(load_rows(coarse_vmem, i, 6), load_rows(coarse_vmem, i, 7))
+
+    loop(0, 8, fill)
+    pl.semaphore_wait(barrier, 14)
+    halos = [
+        remote(units.at[pl.ds(src, count)], got.at[pl.ds(dst, count)], halo_s.at[n], halo_r.at[n], device)
+        for n, (device, src, count, dst) in enumerate(halo_sends)
+    ]
+    for copy in halos:
+        copy.start()
+
+    def row_tile(d, slot):
+        return remote(row_tiles.at[slot], row_tiles.at[slot], tile_s.at[d], tile_r.at[d], at(y, mod4(x + d)))
+
+    def column_tile(d, slot):
+        return remote(row_tiles, tiles.at[slot], tile_s.at[3 + d], tile_r.at[3 + d], at(mod4(y + d), x))
+
+    for d in (1, 2, 3):
+        row_tile(d, x).start()
+    for d in (1, 2, 3):
+        row_tile(d, x).wait_send()
+        row_tile(d, mod4(x - d)).wait_recv()
+    for d in (1, 2, 3):
+        column_tile(d, y).start()
+    tiles[y] = row_tiles[...]
+    for d in (1, 2, 3):
+        column_tile(d, y).wait_send()
+        column_tile(d, mod4(y - d)).wait_recv()
+    lane = lax.broadcasted_iota(jnp.int32, (8, NY), 1)
+    owners = [tiles[i // 4, i % 4] for i in range(PEERS)]
+    pick0 = jnp.full((8, NY), 16, jnp.int32)
+    pick1 = pick0
+    for i in range(PEERS):
+        slot = owners[i] * 2
+        for j in range(i):
+            slot = slot + jnp.where(owners[j] == owners[i], 1, 0)
+        pick0 = jnp.where(slot == lane, i, pick0)
+        pick1 = jnp.where(slot == lane, (i % 4) * 4 + i // 4, pick1)
+    order[0] = pick0
+    order[1] = pick1
+    to_smem = pltpu.make_async_copy(order, order_smem, load_sem)
+    to_smem.start()
+    to_smem.wait()
+    for copy in halos:
+        copy.wait()
+
     edges = [jnp.where(hit, 0.0, 1.0) for hit in (r == 0, r == nr - 1, p == 0, p == np_ - 1)]
-    stage_coarse(coarse_hbm, coarse_vmem, sem).wait()
     fill_rows(coarse_vmem, got, rows, edges)
     gw, aw = gw_ref[...], aw_ref[...]
     build_windows(rows, corner, picks, window, weights)
@@ -332,32 +364,208 @@
     for z in (1, 2, 3):
         once[z] = first_step(ghosted, z, coef, vel, gw, aw)
 
-    def plane(z, _):
+    def send1a(j, q, xj):
+        return remote(packed.at[j, 0], mid0.at[q, x], s1a.at[j], r1a.at[q * 4 + x], at(y, xj))
+
+    def send1b(j, q, yj):
+        return remote(packed.at[j, 1], mid1.at[q, y], s1b.at[j], r1b.at[q * 4 + y], at(yj, x))
+
+    def wait1a(q, sx):
+        remote(packed.at[0, 0], mid0.at[q, sx], s1a.at[0], r1a.at[q * 4 + sx], at(y, sx)).wait_recv()
+
+    def wait1b(q, sy):
+        remote(packed.at[0, 1], mid1.at[q, sy], s1b.at[0], r1b.at[q * 4 + sy], at(sy, x)).wait_recv()
+
+    def send2a(q, yj):
+        return remote(mid0.at[q], held0.at[pl.ds(y * 4, 4)], s2a.at[q], r2a.at[y], at(yj, x))
+
+    def send2b(q, xj):
+        return remote(mid1.at[q], held1.at[pl.ds(x * 4, 4)], s2b.at[q], r2b.at[x], at(y, xj))
+
+    def wait2a(sy):
+        remote(mid0.at[0], held0.at[pl.ds(sy * 4, 4)], s2a.at[0], r2a.at[sy], at(sy, x)).wait_recv()
+
+    def wait2b(sx):
+        remote(mid1.at[0], held1.at[pl.ds(sx * 4, 4)], s2b.at[0], r2b.at[sx], at(y, sx)).wait_recv()
+
+    def send3a(xo):
+        return remote(staged0.at[xo], relay0.at[x], s3a.at[xo], r3a.at[x], at(y, xo))
+
+    def send3b(yo):
+        return remote(staged1.at[yo], relay1.at[y], s3b.at[yo], r3b.at[y], at(yo, x))
+
+    def wait3a(sx):
+        remote(staged0.at[0], relay0.at[sx], s3a.at[0], r3a.at[sx], at(y, sx)).wait_recv()
+
+    def wait3b(sy):
+        remote(staged1.at[0], relay1.at[sy], s3b.at[0], r3b.at[sy], at(sy, x)).wait_recv()
+
+    def send4a(q, yo):
+        sx = mod4(y - q)
+        return remote(relay0.at[sx, yo], landed.at[q * 4 + sx, 0], s4a.at[q * 4 + yo], r4a.at[q * 4 + sx], at(yo, x))
+
+    def send4b(q, xo):
+        sy = mod4(x + q)
+        return remote(relay1.at[sy, xo], landed.at[q * 4 + x, 1], s4b.at[q * 4 + xo], r4b.at[q * 4 + x], at(y, xo))
+
+    def wait4a(j):
+        remote(relay0.at[0, 0], landed.at[j, 0], s4a.at[0], r4a.at[j], at(y, mod4(x + 1))).wait_recv()
+
+    def wait4b(j):
+        remote(relay1.at[0, 0], landed.at[j, 1], s4b.at[0], r4b.at[j], at(mod4(y + 1), x)).wait_recv()
+
+    def plane(q, i):
+        j = q * 4 + i
+        z = j + 2
         second = second_step(once, z, coef, vel, gw, aw)
         chosen = jnp.where(twice, second, once[z]).astype(BF16)
         ahead = jnp.minimum(z + 2, 18)
         once[ahead] = first_step(ghosted, ahead, coef, vel, gw, aw)
         pair = [dot(chosen[:, n * LANES : (n + 1) * LANES], gather[...]) for n in range(2)]
-        packed[z - 2] = pack_pair(*pair)
-        return 0
-
-    lax.fori_loop(2, 18, plane, 0)
-    advance_coarse(rows, coarse_out, coef, vel, gw, aw)
-
-
-def advance(corner, level, vel, coarse, got, cells, coef, gw, aw):
+        chunk = pack_pair(*pair)
+        packed[j, 0] = chunk[:, :NY]
+        packed[j, 1] = chunk[:, NY:]
+        yj = mod4(i + q)
+
+        @pl.when(i == x)
+        def _():
+            mid0[q, x] = packed[j, 0]
+
+        @pl.when(i != x)
+        def _():
+            send1a(j, q, i).start()
+
+        @pl.when(yj == y)
+        def _():
+            mid1[q, y] = packed[j, 1]
+
+        @pl.when(yj != y)
+        def _():
+            send1b(j, q, yj).start()
+
+    def forward(q):
+        for d in (1, 2, 3):
+            wait1a(q, mod4(x + d))
+            wait1b(q, mod4(y + d))
+
+        @pl.when(q == mine)
+        def _():
+            held0[pl.ds(y * 4, 4)] = mid0[q]
+            held1[pl.ds(x * 4, 4)] = mid1[q]
+
+        @pl.when(q != mine)
+        def _():
+            send2a(q, mod4(x + q)).start()
+            send2b(q, mod4(y - q)).start()
+
+    def deal():
+        for d in (1, 2, 3):
+            wait2a(mod4(y + d))
+            wait2b(mod4(x + d))
+
+        def one(d):
+            xo, yo = mod4(x + d), mod4(y + d)
+
+            def copy(n):
+                k, other = lax.rem(n, 2), n // 2
+                staged0[xo, other, k] = held0[order_smem[0, 0, (other * 4 + xo) * 2 + k]]
+                staged1[yo, other, k] = held1[order_smem[1, 0, (yo * 4 + other) * 2 + k]]
+
+            loop(0, 8, copy)
+
+            @pl.when(d > 0)
+            def _():
+                send3a(xo).start()
+                send3b(yo).start()
+
+        loop(1, 4, one)
+        one(0)
+        relay0[x] = staged0[x]
+        relay1[y] = staged1[y]
+
+    def finish(q):
+        sx, sy = mod4(y - q), mod4(x + q)
+
+        @pl.when(q != mine)
+        def _():
+            wait3a(sx)
+            wait3b(sy)
+
+        for d in (1, 2, 3):
+            send4a(q, mod4(y + d)).start()
+            send4b(q, mod4(x + d)).start()
+        landed[q * 4 + sx, 0] = relay0[sx, y]
+        landed[q * 4 + x, 1] = relay1[sy, x]
+
+    def tick(q):
+        @pl.when(q < 4)
+        def _():
+            loop(0, 4, lambda i: plane(q, i))
+
+        @pl.when(jnp.logical_and(q >= 1, q <= 4))
+        def _():
+            forward(q - 1)
+
+        @pl.when(q - 2 == mine)
+        def _():
+            deal()
+
+        @pl.when(q >= 3)
+        def _():
+            finish(q - 3)
+
+        @pl.when(jnp.logical_and(q >= 4, q < 6))
+        def _():
+            advance_coarse(rows, coarse_out, coef, vel, gw, aw, (q - 4) * 8)
+
+    loop(0, 7, tick)
+
+    def drain(j):
+        q, i = j // 4, lax.rem(j, 4)
+        yj = mod4(i + q)
+
+        @pl.when(i != x)
+        def _():
+            send1a(j, q, i).wait_send()
+            wait4b(j)
+
+        @pl.when(yj != y)
+        def _():
+            send1b(j, q, yj).wait_send()
+            wait4a(j)
+
+    loop(0, 16, drain)
+
+    def drain_quarter(q):
+        @pl.when(q != mine)
+        def _():
+            send2a(q, mod4(x + q)).wait_send()
+            send2b(q, mod4(y - q)).wait_send()
+
+        for d in (1, 2, 3):
+            send4a(q, mod4(y + d)).wait_send()
+            send4b(q, mod4(x + d)).wait_send()
+
+    loop(0, 4, drain_quarter)
+    for d in (1, 2, 3):
+        send3a(mod4(x + d)).wait_send()
+        send3b(mod4(y + d)).wait_send()
+
+
+def fused(corner, level, vel, owner, coarse, cells, coef, gw, aw):
     spread = jnp.asarray(spread_matrix(), BF16)
     gather = jnp.asarray(spread_matrix()[:, :LANES].T.copy(), BF16)
     weights = jnp.asarray(interp_weights(), BF16)
     vmem = pl.BlockSpec(memory_space=pltpu.VMEM)
     smem = pl.BlockSpec(memory_space=pltpu.SMEM)
+    dma = pltpu.SemaphoreType.DMA
     return pl.pallas_call(
-        advance_kernel,
+        fused_kernel,
         out_shape=(
             jax.ShapeDtypeStruct((FIELDS * 64, NY), F32),
-            jax.ShapeDtypeStruct((PLANES, UNIT, 256), BF16),
+            jax.ShapeDtypeStruct((PLANES, 2, 2, UNIT, NY), BF16),
         ),
-        in_specs=[smem, smem, smem, pl.BlockSpec(memory_space=pl.ANY)] + [vmem] * 8,
+        in_specs=[smem] * 4 + [pl.BlockSpec(memory_space=pl.ANY)] + [vmem] * 7,
         out_specs=(vmem, vmem),
         scratch_shapes=[
             pltpu.VMEM((ROWS * 64, NY), F32),
@@ -366,92 +574,42 @@
             pltpu.VMEM((2, WIN, ROWS, WIDE), F32),
             pltpu.VMEM((2, EDGE, ROWS, WIDE), F32),
             pltpu.VMEM((EDGE, ROWS, 2 * LANES), F32),
-            pltpu.SemaphoreType.DMA,
+            pltpu.VMEM((32, UNIT, NY), BF16),
+            pltpu.VMEM((40, UNIT, NY), BF16),
+            pltpu.VMEM((4, 8, NY), jnp.int32),
+            pltpu.VMEM((4, 4, 8, NY), jnp.int32),
+            pltpu.VMEM((2, 8, NY), jnp.int32),
+            pltpu.SMEM((2, 8, NY), jnp.int32),
+            pltpu.VMEM((PLANES, 2, UNIT, NY), BF16),
+            pltpu.VMEM((4, 4, UNIT, NY), BF16),
+            pltpu.VMEM((4, 4, UNIT, NY), BF16),
+            pltpu.VMEM((17, UNIT, NY), BF16),
+            pltpu.VMEM((17, UNIT, NY), BF16),
+            pltpu.VMEM((4, 4, 2, UNIT, NY), BF16),
+            pltpu.VMEM((4, 4, 2, UNIT, NY), BF16),
+            pltpu.VMEM((4, 4, 2, UNIT, NY), BF16),
+            pltpu.VMEM((4, 4, 2, UNIT, NY), BF16),
+            dma,
+            dma((8,)), dma((8,)),
+            dma((8,)), dma((8,)),
+            dma((16,)), dma((16,)), dma((16,)), dma((16,)),
+            dma((4,)), dma((4,)), dma((4,)), dma((4,)),
+            dma((4,)), dma((4,)), dma((4,)), dma((4,)),
+            dma((16,)), dma((16,)), dma((16,)), dma((16,)),
         ],
-        compiler_params=pltpu.CompilerParams(vmem_limit_bytes=56 * 1024 * 1024),
-        name="advance",
-    )(corner, level, vel, coarse, got, cells, coef, gw, aw, spread, gather, weights)
-
-
-def exchange_kernel(pick, keep, packed, landed, spread_in, staged, s1, r1, s2, r2):
-    r, p = lax.axis_index("region"), lax.axis_index("patch")
-    barrier = pltpu.get_barrier_semaphore()
-    for d in range(1, PEERS):
-        pl.semaphore_signal(
-            barrier, inc=1, device_id=(r, lax.rem(p + d, PEERS)), device_id_type=MESH
-        )
-    pl.semaphore_wait(barrier, PEERS - 1)
-
-    def first(d):
-        peer = lax.rem(p + d, PEERS)
-        return pltpu.make_async_remote_copy(
-            src_ref=packed.at[peer],
-            dst_ref=spread_in.at[p],
-            send_sem=s1.at[d],
-            recv_sem=r1.at[d],
-            device_id=(r, peer),
-            device_id_type=MESH,
-        )
-
-    def second(d):
-        return pltpu.make_async_remote_copy(
-            src_ref=staged.at[d],
-            dst_ref=landed.at[p],
-            send_sem=s2.at[d],
-            recv_sem=r2.at[d],
-            device_id=(r, lax.rem(p + d, PEERS)),
-            device_id_type=MESH,
-        )
-
-    def each(body):
-        lax.fori_loop(1, PEERS, lambda d, _: (body(d), 0)[1], 0)
-
-    each(lambda d: first(d).start())
-    spread_in[p] = packed[p]
-    each(lambda d: first(d).wait())
-
-    def item(owner, k):
-        n = owner * 2 + k
-        chunk = spread_in[pick[n]]
-        return jnp.where(keep[n] > 0, chunk, jnp.zeros_like(chunk))
-
-    def send(d):
-        owner = lax.rem(p + d, PEERS)
-        for k in range(2):
-            staged[d, k] = item(owner, k)
-        second(d).start()
-
-    each(send)
-    for k in range(2):
-        landed[p, k] = item(p, k)
-    each(lambda d: second(d).wait())
-
-
-def exchange(pick, keep, packed):
-    vmem = pl.BlockSpec(memory_space=pltpu.VMEM)
-    smem = pl.BlockSpec(memory_space=pltpu.SMEM)
-    return pl.pallas_call(
-        exchange_kernel,
-        out_shape=jax.ShapeDtypeStruct((PEERS, 2, UNIT, 256), BF16),
-        in_specs=[smem, smem, vmem],
-        out_specs=vmem,
-        scratch_shapes=[
-            pltpu.VMEM((PEERS, UNIT, 256), BF16),
-            pltpu.VMEM((PEERS, 2, UNIT, 256), BF16),
-        ]
-        + [pltpu.SemaphoreType.DMA((PEERS,))] * 4,
         compiler_params=pltpu.CompilerParams(
-            collective_id=1, has_side_effects=True, vmem_limit_bytes=32 * 1024 * 1024
+            collective_id=0, has_side_effects=True, vmem_limit_bytes=60 * 1024 * 1024
         ),
-        name="exchange",
-    )(pick, keep, packed)
+        name="fused",
+    )(corner, level, vel, owner, coarse, cells, coef, gw, aw, spread, gather, weights)
 
 
 def place_kernel(landed, out):
     for j in range(PLANES):
-        first, second = unpack_pair(landed[j, 0])
-        out[0, :, pl.ds(j * 256, 256)] = first[:FIELDS].astype(BF16)
-        out[1, :, pl.ds(j * 256, 256)] = second[:FIELDS].astype(BF16)
+        for h in range(2):
+            first, second = unpack_pair(landed[j, h, 0])
+            out[0, :, pl.ds(j * 256 + h * NY, NY)] = first[:FIELDS].astype(BF16)
+            out[1, :, pl.ds(j * 256 + h * NY, NY)] = second[:FIELDS].astype(BF16)
 
 
 def place(landed):
@@ -459,7 +617,7 @@
         place_kernel,
         grid=(2,),
         out_shape=jax.ShapeDtypeStruct((4, FIELDS, B**3), BF16),
-        in_specs=[pl.BlockSpec((PLANES, 1, UNIT, 256), lambda k: (0, k, 0, 0))],
+        in_specs=[pl.BlockSpec((PLANES, 2, 1, UNIT, NY), lambda k: (0, 0, k, 0, 0))],
         out_specs=pl.BlockSpec((2, FIELDS, B**3), lambda k: (k, 0, 0)),
         name="place",
     )(landed)
@@ -488,18 +646,11 @@
 def shards(
     coarse, fine_patches, new_owner, corners, level_tags, diffusivity, velocity, growth_weight, yield_weight
 ):
-    owners = lax.all_gather(new_owner[:1, 0], "patch", tiled=True)
-    before = jnp.arange(PEERS)[None, :] < jnp.arange(PEERS)[:, None]
-    rank = jnp.sum((owners[:, None] == owners[None, :]) & before, axis=1)
-    slot = owners * 2 + rank
-    match = slot[None, :] == jnp.arange(2 * PEERS)[:, None]
-    pick = jnp.sum(jnp.where(match, jnp.arange(PEERS)[None, :], 0), axis=1)
-    keep = jnp.any(match, axis=1).astype(jnp.int32)
     coef, vel, gw, aw = parameters(diffusivity, velocity, growth_weight, yield_weight)
     flat = coarse.reshape(FIELDS * 64, NY)
-    got = halo(flat)
-    coarse_next, packed = advance(corners[:, 2], level_tags, vel, flat, got, fine_patches, coef, gw, aw)
-    landed = exchange(pick, keep, packed)
+    coarse_next, landed = fused(
+        corners[:, 2], level_tags, vel, new_owner[:1, 0], flat, fine_patches, coef, gw, aw
+    )
     return coarse_next.reshape(coarse.shape), place(landed)
 
 

time: 148 us -> 126 us (0.85)
  the two profiles are of different devices: /device:TPU:6 before, /device:TPU:100 now
where the time goes in v2:
time: 126 us
  Pallas kernels  106 us (84%)
  local copies, waits for them, and re-layouts  12.3 us (10%)
  other arithmetic  6.06 us (5%)
  between operations  1.31 us (1%)
    pallas_call x1, Pallas kernels, fused(): pl.pallas_call(fused_kernel, out_shape=(jax.ShapeDtypeStruct((FIELDS * 64...  103 us
    unnamed x6, local copies, waits for them, and re-layouts  10.1 us
    pallas_call x1, Pallas kernels, place(): pl.pallas_call(place_kernel, grid=(2,), out_shape=jax.ShapeDtypeStruct((4...  3.01 us

profile of v2, /device:TPU:100, one launch (start us, length us, event | category | flops | bytes accessed | tf_op | source)
XLA Modules:
  0.0 125.7 jit_solution(12444873030395880130)
XLA Ops:
  0.6 1.4 %slice_reduce_fusion.corner = s32[2]{0:T(128)} fusion(s32[2,3]{1,0:T(2,128)} %param.15), kind=kLoop, calls=%fused_computation.13 | loop fusion | bytes 16 | tf_op jit(solution)/shard_map/slice | solution.py:652
  2.1 0.1 pad.15.clone
  2.2 1.3 %fusion.2 = (f32[]{:T(128)}, f32[3]{0:T(128)S(1)}) fusion(f32[3]{0:T(128)} %param.18), kind=kLoop, calls=%fused_computation.21 | loop fusion | flops 5 | bytes 28 | tf_op jit(solution)/shard_map/reduce_sum | solution.py:632
  4.1 1.2 pad_maximum_fusion.3.vel
  5.3 1.3 %subtract_bitcast_fusion.1 = (f32[1,72]{1,0:T(1,128)S(1)}, f32[1,72]{1,0:T(1,128)S(1)}, f32[1,72]{1,0:T(1,128)S(1)}, f32[1,72]{1,0:T(1,128)S(1)}) fusion(f32[]{:T(128)} %get-tuple-element.16, f32[70]{0:T(128)} %param.17, f32[]{:T(128)S(6)} %mul.35), kind=kLoop, calls=%fused_computation.18 | loop fusion | flops 504 | bytes 1440 | tf_op jit(solution)/shard_map/stack | solution.py:634
  6.6 0.1 convert_subtract_fusion
  6.7 0.8 reduce-precision_convert_fusion
  7.5 0.7 pad_maximum_fusion.aw_ref
  8.2 0.8 copy.14
  9.0 0.7 pad_maximum_fusion.1.gw_ref
  9.7 0.8 broadcast_in_dim.4.coef
  10.4 2.9 %copy.15.cells = bf16[2,70,4096]{2,1,0:T(8,128)(2,1)} copy(bf16[2,70,4096]{2,0,1:T(2,128)(2,1)} %param.13) | data formatting | bytes 2293760 | tf_op args[1]
  13.3 103.0 %fused.1 = (f32[4480,128]{1,0:T(8,128)}, bf16[16,2,2,144,128]{4,3,2,1,0:T(8,128)(2,1)}) custom-call(s32[2]{0:T(128)} %slice_reduce_fusion.corner, s32[2]{0:T(128)} %level.1, f32[6]{0:T(128)} %pad_maximum_fusion.3.vel, s32[1]{0:T(128)} %bitcast.14, f32[4480,128]{1,0:T(8,128)} %bitcast.12, bf16[2,70,4096]{2,1,0:T(8,128)(2,1)} %copy.15.cells, ...), custom_call_target="tpu_custom_call" | custom-call | tf_op jit(solution)/shard_map/fused/pallas_call | solution.py:562
  116.3 3.0 %place.1 = bf16[4,70,4096]{2,1,0:T(8,128)(2,1)} custom-call(bf16[16,2,2,144,128]{4,3,2,1,0:T(8,128)(2,1)} %get-tuple-element.5.landed), custom_call_target="tpu_custom_call" | custom-call | tf_op jit(solution)/shard_map/place/pallas_call | solution.py:616
  119.3 0.0 copy-start
  119.3 5.0 %copy.16 = bf16[4,70,4096]{2,0,1:T(4,128)(2,1)} copy(bf16[4,70,4096]{2,1,0:T(8,128)(2,1)} %place.1) | data formatting | bytes 4587520
  124.3 0.0 copy-done
  124.3 1.4 %copy.18 = f32[70,8,8,128]{3,2,1,0:T(8,128)} copy(f32[70,8,8,128]{3,2,1,0:T(8,128)S(1)} %bitcast.13) | data formatting | bytes 4587520
  (4 shorter events, 0.0 us)
Async XLA Ops:
  119.3 5.0 %copy-start = (f32[4480,128]{1,0:T(8,128)S(1)}, f32[4480,128]{1,0:T(8,128)}, u32[]{:S(2)}) copy-start(f32[4480,128]{1,0:T(8,128)} %get-tuple-element.4) | copy-start | bytes 6881284

commit v3 on v1

v3 whole, which is shorter than its diff:
```python
import functools

import jax
import jax.numpy as jnp
import numpy as np
from jax import lax
from jax.experimental import pallas as pl
from jax.experimental.pallas import tpu as pltpu
from jax.sharding import PartitionSpec as P

B = 16
SOOT = 40
SPEC = 30
FIELDS = 70
ROWS = 72
WIN = 12
EDGE = 20
LANES = 384
WIDE = 512
NY = 128
PLANES = 16
PEERS = 16
UNIT = 144
MESH = pl.DeviceIdType.MESH
NEAR = (
    (0, 1), (0, 3), (1, 0), (3, 0), (0, 2), (1, 1), (1, 3), (2, 0),
    (3, 1), (3, 3), (1, 2), (2, 1), (2, 3), (3, 2), (2, 2),
)
F32 = jnp.float32
BF16 = jnp.bfloat16


def spread_matrix():
    e = np.zeros((B * B, WIDE), np.float32)
    for x in range(B):
        for y in range(B):
            e[x * B + y, (x + 2) * EDGE + y + 2] = 1.0
    return e


def interp_weights():
    m = np.zeros((EDGE, WIN), np.float32)
    for f in range(EDGE):
        parent = f // 2 + 1
        m[f, parent] = 0.75
        m[f, parent + (-1 if f % 2 == 0 else 1)] = 0.25
    v = np.zeros((256, WIDE), np.float32)
    for x in range(WIN):
        for y in range(WIN):
            v[16 * x + y, : EDGE * EDGE] = np.outer(m[:, x], m[:, y]).reshape(-1)
    return v


def dot(a, b):
    return lax.dot_general(a, b, (((1,), (0,)), ((), ())), preferred_element_type=F32)


def pack_pair(a, b):
    return jnp.concatenate([a[:64], b[:64], a[64:ROWS], b[64:ROWS]], axis=0).astype(BF16)


def unpack_pair(u):
    u = u.astype(F32)
    first = jnp.concatenate([u[:64], u[128:136]], axis=0)
    second = jnp.concatenate([u[64:128], u[136:144]], axis=0)
    return first, second


def growth(moved, gw, aw):
    soot = moved[:SOOT]
    spec = moved[SOOT:]
    sh = spec.astype(BF16)
    sl = (spec - sh.astype(F32)).astype(BF16)
    pre = dot(gw, jnp.concatenate([sh, sl, sh], axis=0))
    rate = 0.5 * jnp.tanh(0.5 * pre) + 0.5
    flux = rate * soot
    fh = flux.astype(BF16).astype(F32)
    fl = flux - fh
    return moved + dot(aw, jnp.concatenate([fh, fl, fh], axis=0).astype(BF16))


def tiled(a, n):
    return jnp.concatenate([a] * n, axis=1)


def moved_terms(c, lz, uz, lx, ux, ly, uy, own, diff, v):
    total = (lz + uz) + (lx + ux) + (ly + uy)
    return own * c + diff * total + (v[0] * lz + v[1] * lx + v[2] * ly)


def load_rows(coarse_vmem, z, x):
    return coarse_vmem[pl.ds(z * 8 + x, ROWS, stride=64), :]


def stage_coarse(coarse_hbm, coarse_vmem, sem):
    copy = pltpu.make_async_copy(coarse_hbm, coarse_vmem.at[pl.ds(0, FIELDS * 64)], sem)
    copy.start()
    coarse_vmem[FIELDS * 64 :, :] = jnp.zeros((ROWS * 64 - FIELDS * 64, NY), F32)
    return copy


def fill_rows(coarse_vmem, got, rows, edges):
    z_low, z_high, x_low, x_high = edges

    def own(z, _):
        for x in range(8):
            rows[z + 2, :, pl.ds((x + 2) * NY, NY)] = load_rows(coarse_vmem, z, x)
        a, b = unpack_pair(got[16 + z])
        rows[z + 2, :, pl.ds(0, NY)] = a * x_low
        rows[z + 2, :, pl.ds(NY, NY)] = b * x_low
        a, b = unpack_pair(got[24 + z])
        rows[z + 2, :, pl.ds(10 * NY, NY)] = a * x_high
        rows[z + 2, :, pl.ds(11 * NY, NY)] = b * x_high
        return 0

    lax.fori_loop(0, 8, own, 0)
    for x in range(WIN):
        if x < 2:
            low, high, side = 32 + x, 36 + x, x_low
        elif x < 10:
            low, high, side = x - 2, 8 + x - 2, 1.0
        else:
            low, high, side = 34 + x - 10, 38 + x - 10, x_high
        for unit, z, scale in ((low, 0, z_low * side), (high, 10, z_high * side)):
            a, b = unpack_pair(got[unit])
            rows[z, :, pl.ds(x * NY, NY)] = a * scale
            rows[z + 1, :, pl.ds(x * NY, NY)] = b * scale


def advance_coarse(rows, out, coef, vel, gw, aw, first, last):
    width = 4 * NY
    lane = lax.broadcasted_iota(jnp.int32, (ROWS, width), 1) % NY

    def step(i, _):
        z = i // 2 + 2
        base = pl.multiple_of((i % 2) * width, width)

        def part(dz, dx):
            return rows[z + dz, :, pl.ds(pl.multiple_of(base + (2 + dx) * NY, NY), width)]

        c = part(0, 0)
        pieces = [c[:, n * NY : (n + 1) * NY] for n in range(4)]
        ly = jnp.concatenate([pltpu.roll(t, 1, 1) for t in pieces], axis=1)
        uy = jnp.concatenate([pltpu.roll(t, NY - 1, 1) for t in pieces], axis=1)
        ly = jnp.where(lane == 0, 0.0, ly)
        uy = jnp.where(lane == NY - 1, 0.0, uy)
        moved = moved_terms(
            c, part(-1, 0), part(1, 0), part(0, -1), part(0, 1), ly, uy,
            tiled(coef[2], 4), tiled(coef[3], 4), (0.5 * vel[0], 0.5 * vel[1], 0.5 * vel[2]),
        )
        new = growth(moved, gw, aw)
        for n in range(4):
            at = (z - 2) * 8 + (i % 2) * 4 + n
            out[pl.ds(at, FIELDS, stride=64), :] = new[:FIELDS, n * NY : (n + 1) * NY]
        return 0

    lax.fori_loop(first, last, step, 0)


def build_windows(rows, corner, picks, window, weights):
    lane = lax.broadcasted_iota(jnp.int32, (NY, 256), 1)
    row = lax.broadcasted_iota(jnp.int32, (NY, 256), 0)
    start = jnp.where(lane < NY, corner[0, 2], corner[1, 2]) - 2
    slot = lane % NY
    for x in range(8):
        at = slot - 16 * x
        hit = jnp.logical_and(jnp.logical_and(at >= 0, at < WIN), row == start + at)
        picks[pl.ds(x * NY, NY), :] = jnp.where(hit, 1.0, 0.0).astype(BF16)
    v = weights[...]

    def group(g, _):
        z = g * 3
        lhs = rows[pl.ds(z, 3)].reshape(3 * ROWS, WIN * NY).astype(BF16)
        first = dot(lhs[:, : 8 * NY], picks[...]).astype(BF16)
        second = dot(lhs[:, 8 * NY :], picks[: 4 * NY, :]).astype(BF16)
        for n in range(2):
            cut = slice(n * NY, (n + 1) * NY)
            both = jnp.concatenate([first[:, cut], second[:, cut]], axis=1)
            window[n, pl.ds(z, 3)] = dot(both, v).reshape(3, ROWS, WIDE)
        return 0

    lax.fori_loop(0, 4, group, 0)


def build_ghosted(window, cells, ghosted, spread):
    lane = lax.broadcasted_iota(jnp.int32, (ROWS, WIDE), 1)
    x, y = lane // EDGE, lane % EDGE
    inside = (x >= 2) & (x < 18) & (y >= 2) & (y < 18)
    e = spread[...]
    pad = jnp.zeros((ROWS - FIELDS, 256), F32)

    def blend(n, f, parent, other):
        return 0.75 * window[n, parent] + 0.25 * window[n, other]

    for n in range(2):
        for f in (0, 1, 18, 19):
            parent = f // 2 + 1
            ghosted[n, f] = blend(n, f, parent, parent + (-1 if f % 2 == 0 else 1))

    def group(g, _):
        for n in range(2):
            planes = []
            for k in range(4):
                at = pl.multiple_of((g * 4 + k) * 256, 256)
                planes.append(jnp.concatenate([cells[n, :, pl.ds(at, 256)].astype(F32), pad], axis=0))
            full = dot(jnp.concatenate(planes, axis=0).astype(BF16), e)
            for k in range(4):
                f = 2 + g * 4 + k
                parent = 2 + g * 2 + k // 2
                other = parent + (-1 if k % 2 == 0 else 1)
                ghosted[n, f] = jnp.where(inside, full[k * ROWS : (k + 1) * ROWS], blend(n, f, parent, other))
        return 0

    lax.fori_loop(0, 4, group, 0)


def first_step(ghosted, z, coef, vel, gw, aw):
    moved = []
    for n in range(2):
        wide = ghosted[n, z]
        c = wide[:, :LANES]
        moved.append(
            moved_terms(
                c,
                ghosted[n, z - 1, :, :LANES],
                ghosted[n, z + 1, :, :LANES],
                pltpu.roll(c, EDGE, 1),
                pltpu.roll(wide, WIDE - EDGE, 1)[:, :LANES],
                pltpu.roll(c, 1, 1),
                pltpu.roll(c, LANES - 1, 1),
                tiled(coef[0], 3), tiled(coef[1], 3), (vel[0], vel[1], vel[2]),
            )
        )
    return growth(jnp.concatenate(moved, axis=1), gw, aw)


def second_step(once, z, coef, vel, gw, aw):
    moved = []
    for n in range(2):
        cut = pl.ds(n * LANES, LANES)
        c = once[z, :, cut]
        moved.append(
            moved_terms(
                c,
                once[z - 1, :, cut],
                once[z + 1, :, cut],
                pltpu.roll(c, EDGE, 1),
                pltpu.roll(c, LANES - EDGE, 1),
                pltpu.roll(c, 1, 1),
                pltpu.roll(c, LANES - 1, 1),
                tiled(coef[0], 3), tiled(coef[1], 3), (vel[0], vel[1], vel[2]),
            )
        )
    return growth(jnp.concatenate(moved, axis=1), gw, aw)


def remote(src, dst, send, recv, device):
    return pltpu.make_async_remote_copy(
        src_ref=src, dst_ref=dst, send_sem=send, recv_sem=recv, device_id=device, device_id_type=MESH
    )


def loop(start, stop, body):
    lax.fori_loop(start, stop, lambda i, _: (body(i), 0)[1], 0)


def prepare(diff_ref, vel, grow_ref, yield_ref, coef, grow_pad, yield_pad):
    lane = lax.broadcasted_iota(jnp.int32, (ROWS, NY), 1)
    row = lax.broadcasted_iota(jnp.int32, (ROWS, NY), 0)
    flat = jnp.concatenate([diff_ref[...], jnp.zeros((1, NY - FIELDS), F32)], axis=1)
    spread = jnp.where(lane == row, jnp.broadcast_to(flat, (ROWS, NY)), 0.0)
    d = jnp.broadcast_to(jnp.sum(spread, axis=1, keepdims=True), (ROWS, NY))
    flow = vel[0] + vel[1] + vel[2]
    coef[0] = 1.0 - 6.0 * d - flow
    coef[1] = d
    coef[2] = 1.0 - 1.5 * d - 0.5 * flow
    coef[3] = 0.25 * d
    grow_pad[...] = jnp.zeros_like(grow_pad)
    grow_pad[:SPEC, :SOOT] = grow_ref[...]
    g = jnp.transpose(grow_pad[...])[:SOOT]
    gh = g.astype(BF16).astype(F32)
    gw = jnp.concatenate([gh, gh, g - gh], axis=1).astype(BF16)
    yield_pad[...] = jnp.zeros_like(yield_pad)
    yield_pad[SOOT:FIELDS, :SOOT] = yield_ref[...]
    change = jnp.where(row == lane + 1, 1.0, 0.0) - jnp.where(row == lane, 1.0, 0.0)
    a = 0.5 * jnp.where(row < SOOT, change, yield_pad[...])[:, :SOOT]
    ah = a.astype(BF16).astype(F32)
    aw = jnp.concatenate([ah, ah, a - ah], axis=1).astype(BF16)
    return gw, aw


def offset(c):
    return (15 - c) // 4, lax.rem(15 - c, 4)


def fused_kernel(
    corner, level, vel, owner, coarse_hbm, cells, diff_ref, grow_ref, yield_ref, spread, gather, weights,
    coarse_out, landed, order_out,
    coarse_vmem, rows, picks, window, ghosted, once, coef, grow_pad, yield_pad,
    units, got, tiles, order, order_smem, packed, held, staged,
    load_sem, halo_s, halo_r, tile_s, tile_r, spread_s, spread_r, deal_s, deal_r,
):
    r, p = lax.axis_index("region"), lax.axis_index("patch")
    nr, np_ = lax.axis_size("region"), lax.axis_size("patch")
    y, x = p // 4, lax.rem(p, 4)
    up_r, down_r = lax.rem(r + 1, nr), lax.rem(r + nr - 1, nr)
    up_p, down_p = lax.rem(p + 1, np_), lax.rem(p + np_ - 1, np_)

    def peer(dy, dx):
        return lax.rem(y + dy, 4) * 4 + lax.rem(x + dx, 4)

    halo_sends = [
        ((up_r, p), 8, 8, 0),
        ((down_r, p), 0, 8, 8),
        ((r, up_p), 24, 8, 16),
        ((r, down_p), 16, 8, 24),
        ((up_r, up_p), 14, 2, 32),
        ((up_r, down_p), 8, 2, 34),
        ((down_r, up_p), 6, 2, 36),
        ((down_r, down_p), 0, 2, 38),
    ]
    barrier = pltpu.get_barrier_semaphore()
    for device, _, _, _ in halo_sends:
        pl.semaphore_signal(barrier, inc=1, device_id=device, device_id_type=MESH)

    def greet(d):
        pl.semaphore_signal(barrier, inc=1, device_id=(r, lax.rem(p + d, PEERS)), device_id_type=MESH)

    loop(1, PEERS, greet)
    load = stage_coarse(coarse_hbm, coarse_vmem, load_sem)
    tiles[p] = jnp.full((8, NY), owner[0, 0], jnp.int32)
    held[16] = jnp.zeros((UNIT, 256), BF16)
    gw, aw = prepare(diff_ref, vel, grow_ref, yield_ref, coef, grow_pad, yield_pad)
    load.wait()

    def fill(i):
        units[i] = pack_pair(load_rows(coarse_vmem, 0, i), load_rows(coarse_vmem, 1, i))
        units[8 + i] = pack_pair(load_rows(coarse_vmem, 6, i), load_rows(coarse_vmem, 7, i))
        units[16 + i] = pack_pair(load_rows(coarse_vmem, i, 0), load_rows(coarse_vmem, i, 1))
        units[24 + i] = pack_pair(load_rows(coarse_vmem, i, 6), load_rows(coarse_vmem, i, 7))

    loop(0, 8, fill)
    pl.semaphore_wait(barrier, 8 + PEERS - 1)
    halos = [
        remote(units.at[pl.ds(src, count)], got.at[pl.ds(dst, count)], halo_s.at[n], halo_r.at[n], device)
        for n, (device, src, count, dst) in enumerate(halo_sends)
    ]
    for copy in halos:
        copy.start()

    def tile(d, slot):
        return remote(tiles.at[slot], tiles.at[slot], tile_s.at[d], tile_r.at[d], (r, lax.rem(p + d, PEERS)))

    loop(1, PEERS, lambda d: tile(d, p).start())
    for copy in halos:
        copy.wait()

    edges = [jnp.where(hit, 0.0, 1.0) for hit in (r == 0, r == nr - 1, p == 0, p == np_ - 1)]
    fill_rows(coarse_vmem, got, rows, edges)
    build_windows(rows, corner, picks, window, weights)
    build_ghosted(window, cells, ghosted, spread)
    lane = lax.broadcasted_iota(jnp.int32, (ROWS, 2 * LANES), 1)
    twice = jnp.where(lane < LANES, level[0], level[1]) == 2
    for z in (1, 2, 3):
        once[z] = first_step(ghosted, z, coef, vel, gw, aw)

    def give(c):
        return remote(packed.at[c], held.at[p], spread_s.at[c], spread_r.at[c], (r, peer(*offset(c))))

    def take(c):
        dy, dx = offset(c)
        source = peer(4 - dy, 4 - dx)
        remote(packed.at[c], held.at[source], spread_s.at[c], spread_r.at[c], (r, source)).wait_recv()

    def plane(c):
        z = c + 2
        second = second_step(once, z, coef, vel, gw, aw)
        chosen = jnp.where(twice, second, once[z]).astype(BF16)
        ahead = jnp.minimum(z + 2, 18)
        once[ahead] = first_step(ghosted, ahead, coef, vel, gw, aw)
        pair = [dot(chosen[:, n * LANES : (n + 1) * LANES], gather[...]) for n in range(2)]
        packed[c] = pack_pair(*pair)

        @pl.when(c < 15)
        def _():
            give(c).start()

    loop(0, PLANES, plane)
    held[p] = packed[15]
    advance_coarse(rows, coarse_out, coef, vel, gw, aw, 0, 4)

    def settle(d):
        tile(d, p).wait_send()
        tile(d, lax.rem(p + PEERS - d, PEERS)).wait_recv()

    loop(1, PEERS, settle)
    lane = lax.broadcasted_iota(jnp.int32, (8, NY), 1)
    owners = [tiles[i] for i in range(PEERS)]
    pick = jnp.full((8, NY), 16, jnp.int32)
    for i in range(PEERS):
        slot = owners[i] * 2
        for j in range(i):
            slot = slot + jnp.where(owners[j] == owners[i], 1, 0)
        pick = jnp.where(slot == lane, i, pick)
    order[...] = pick
    order_out[...] = pick
    to_smem = pltpu.make_async_copy(order, order_smem, load_sem)
    to_smem.start()
    to_smem.wait()
    loop(0, 15, take)

    def deal(n, dy, dx):
        return remote(staged.at[n], landed.at[p], deal_s.at[n], deal_r.at[n], (r, peer(dy, dx)))

    for n, (dy, dx) in enumerate(NEAR):
        for k in range(2):
            staged[n, k] = held[order_smem[0, peer(dy, dx) * 2 + k]]
        deal(n, dy, dx).start()
    for k in range(2):
        landed[p, k] = held[order_smem[0, p * 2 + k]]
    advance_coarse(rows, coarse_out, coef, vel, gw, aw, 4, 16)
    loop(0, 15, lambda c: give(c).wait_send())
    for n, (dy, dx) in enumerate(NEAR):
        deal(n, dy, dx).wait_send()
        source = peer(4 - dy, 4 - dx)
        remote(staged.at[n], landed.at[source], deal_s.at[n], deal_r.at[n], (r, source)).wait_recv()


def fused(corner, level, vel, owner, coarse, cells, diff, grow, give):
    spread = jnp.asarray(spread_matrix(), BF16)
    gather = jnp.asarray(spread_matrix()[:, :LANES].T.copy(), BF16)
    weights = jnp.asarray(interp_weights(), BF16)
    vmem = pl.BlockSpec(memory_space=pltpu.VMEM)
    smem = pl.BlockSpec(memory_space=pltpu.SMEM)
    dma = pltpu.SemaphoreType.DMA
    return pl.pallas_call(
        fused_kernel,
        out_shape=(
            jax.ShapeDtypeStruct((FIELDS * 64, NY), F32),
            jax.ShapeDtypeStruct((PEERS, 2, UNIT, 256), BF16),
            jax.ShapeDtypeStruct((8, NY), jnp.int32),
        ),
        in_specs=[smem] * 4 + [pl.BlockSpec(memory_space=pl.ANY)] + [vmem] * 7,
        out_specs=(vmem, vmem, vmem),
        scratch_shapes=[
            pltpu.VMEM((ROWS * 64, NY), F32),
            pltpu.VMEM((WIN, ROWS, WIN * NY), F32),
            pltpu.VMEM((8 * NY, 256), BF16),
            pltpu.VMEM((2, WIN, ROWS, WIDE), F32),
            pltpu.VMEM((2, EDGE, ROWS, WIDE), F32),
            pltpu.VMEM((EDGE, ROWS, 2 * LANES), F32),
            pltpu.VMEM((4, ROWS, NY), F32),
            pltpu.VMEM((32, NY), F32),
            pltpu.VMEM((ROWS, NY), F32),
            pltpu.VMEM((32, UNIT, NY), BF16),
            pltpu.VMEM((40, UNIT, NY), BF16),
            pltpu.VMEM((PEERS, 8, NY), jnp.int32),
            pltpu.VMEM((8, NY), jnp.int32),
            pltpu.SMEM((8, NY), jnp.int32),
            pltpu.VMEM((PLANES, UNIT, 256), BF16),
            pltpu.VMEM((17, UNIT, 256), BF16),
            pltpu.VMEM((15, 2, UNIT, 256), BF16),
            dma,
            dma((8,)), dma((8,)), dma((16,)), dma((16,)), dma((16,)), dma((16,)), dma((15,)), dma((15,)),
        ],
        compiler_params=pltpu.CompilerParams(
            collective_id=0, has_side_effects=True, vmem_limit_bytes=60 * 1024 * 1024
        ),
        name="fused",
    )(corner, level, vel, owner, coarse, cells, diff, grow, give, spread, gather, weights)


def place_kernel(order, landed, out):
    p = lax.axis_index("patch")
    step = pl.program_id(0)
    for i in range(4):
        dy, dx = offset(step * 4 + i)
        four = []
        for k in range(2):
            item = jnp.minimum(order[0, p * 2 + k], PEERS - 1)
            handler = lax.rem(item // 4 + dy, 4) * 4 + lax.rem(item + dx, 4)
            four.extend(unpack_pair(landed[handler, k]))
        out[:, :, pl.ds(i * 256, 256)] = jnp.stack([f[:FIELDS] for f in four], axis=1).astype(BF16)


def place(order, landed):
    return pl.pallas_call(
        place_kernel,
        grid=(4,),
        out_shape=jax.ShapeDtypeStruct((FIELDS, 4, B**3), BF16),
        in_specs=[
            pl.BlockSpec(memory_space=pltpu.SMEM),
            pl.BlockSpec((PEERS, 2, UNIT, 256), lambda k: (0, 0, 0, 0)),
        ],
        out_specs=pl.BlockSpec((FIELDS, 4, 1024), lambda k: (0, 0, k)),
        compiler_params=pltpu.CompilerParams(vmem_limit_bytes=32 * 1024 * 1024),
        name="place",
    )(order, landed)


def shards(
    coarse, fine_patches, new_owner, corners, level_tags, diffusivity, velocity, growth_weight, yield_weight
):
    coarse_next, landed, order = fused(
        corners, level_tags, velocity, new_owner, coarse.reshape(FIELDS * 64, NY), fine_patches,
        diffusivity[None, :], growth_weight.T, yield_weight,
    )
    fine_next = jnp.transpose(place(order, landed), (1, 0, 2))
    return coarse_next.reshape(coarse.shape), fine_next


def solution(mesh):
    placed = (
        P(None, "region", "patch", None),
        P(("region", "patch"), None, None),
        P(("region", "patch"), None),
        P(("region", "patch"), None),
        P(("region", "patch")),
        P(),
        P(),
        P(),
        P(),
    )
    return jax.shard_map(
        shards,
        mesh=mesh,
        in_specs=placed,
        out_specs=(P(None, "region", "patch", None), P(("region", "patch"), None, None)),
        check_vma=False,
    )
```

time: 148 us -> 98.9 us (0.67)
  the two profiles are of different devices: /device:TPU:6 before, /device:TPU:112 now
where the time goes in v3:
time: 98.9 us; the launch traced here: 98.6 us
  Pallas kernels  90.1 us (91%)
  local copies, waits for them, and re-layouts  7.92 us (8%)
    pallas_call x1, Pallas kernels, fused(): pl.pallas_call(fused_kernel, out_shape=(jax.ShapeDtypeStruct((FIELDS * 64...  85.1 us
    unnamed x9, local copies, waits for them, and re-layouts  7.92 us
    pallas_call x1, Pallas kernels, place(): pl.pallas_call(place_kernel, grid=(4,), out_shape=jax.ShapeDtypeStruct((F...  5 us

profile of v3, /device:TPU:112, one launch (start us, length us, event | category | flops | bytes accessed | tf_op | source)
XLA Modules:
  0.0 98.6 jit_solution(12548976194849537343)
XLA Ops:
  0.6 1.3 %copy.14.owner = s32[2,1]{1,0:T(2,128)} copy(s32[2,1]{0,1:T(1,128)} %param.14) | data formatting | bytes 16 | tf_op args[2]
  1.9 2.9 %copy.15.cells = bf16[2,70,4096]{2,1,0:T(8,128)(2,1)} copy(bf16[2,70,4096]{2,0,1:T(2,128)(2,1)} %param.13) | data formatting | bytes 2293760 | tf_op args[1]
  4.8 85.1 %fused.1 = (f32[4480,128]{1,0:T(8,128)}, bf16[16,2,144,256]{3,2,1,0:T(8,128)(2,1)}, s32[8,128]{1,0:T(8,128)}) custom-call(s32[2,3]{1,0:T(2,128)} %corner.1, s32[2]{0:T(128)} %level.1, f32[3]{0:T(128)} %vel.1, s32[2,1]{1,0:T(2,128)} %copy.14.owner, f32[4480,128]{1,0:T(8,128)} %bitcast.5, bf16[2,70,4096]{2,1,0:T(8,128)(2,1)} %copy.15.cells, f32[1,70]{1,0:T(1,128)} %bitcast.9, ...), custom_call_target="tpu_custom_call" | custom-call | tf_op jit(solution)/shard_map/fused/pallas_call | solution.py:436
  89.9 0.0 copy-start
  89.9 1.7 %copy-done = bf16[16,2,144,256]{3,2,1,0:T(8,128)(2,1)S(1)} copy-done((bf16[16,2,144,256]{3,2,1,0:T(8,128)(2,1)S(1)}, bf16[16,2,144,256]{3,2,1,0:T(8,128)(2,1)}, u32[]{:S(2)}) %copy-start) | copy-done | bytes 2359320
  91.6 0.0 copy-start.1
  91.6 0.7 copy-done.1
  92.2 0.0 copy-start.2
  92.2 5.0 %place.1 = bf16[70,4,4096]{2,1,0:T(4,128)(2,1)} custom-call(s32[8,128]{1,0:T(8,128)S(1)} %copy-done.1, bf16[16,2,144,256]{3,2,1,0:T(8,128)(2,1)S(1)} %copy-done), custom_call_target="tpu_custom_call" | custom-call | tf_op jit(solution)/shard_map/place/pallas_call | solution.py:487
  97.2 0.0 copy-done.2
  97.2 1.4 %copy.17 = f32[70,8,8,128]{3,2,1,0:T(8,128)} copy(f32[70,8,8,128]{3,2,1,0:T(8,128)S(1)} %bitcast.6) | data formatting | bytes 4587520
Async XLA Ops:
  89.9 1.7 %copy-start = (bf16[16,2,144,256]{3,2,1,0:T(8,128)(2,1)S(1)}, bf16[16,2,144,256]{3,2,1,0:T(8,128)(2,1)}, u32[]{:S(2)}) copy-start(bf16[16,2,144,256]{3,2,1,0:T(8,128)(2,1)} %get-tuple-element.7.landed) | copy-start | bytes 7077892
  91.6 0.7 copy-start.1
  92.2 5.0 %copy-start.2 = (f32[4480,128]{1,0:T(8,128)S(1)}, f32[4480,128]{1,0:T(8,128)}, u32[]{:S(2)}) copy-start(f32[4480,128]{1,0:T(8,128)} %get-tuple-element.5) | copy-start | bytes 6881284

commit v4 on v3

--- a/solution.py
+++ b/solution.py
@@ -22,10 +22,6 @@
 PEERS = 16
 UNIT = 144
 MESH = pl.DeviceIdType.MESH
-NEAR = (
-    (0, 1), (0, 3), (1, 0), (3, 0), (0, 2), (1, 1), (1, 3), (2, 0),
-    (3, 1), (3, 3), (1, 2), (2, 1), (2, 3), (3, 2), (2, 2),
-)
 F32 = jnp.float32
 BF16 = jnp.bfloat16
 
@@ -182,12 +178,29 @@
     lax.fori_loop(0, 4, group, 0)
 
 
-def build_ghosted(window, cells, ghosted, spread):
+def expand(cells, ghosted, spread):
+    e = spread[...]
+    pad = jnp.zeros((ROWS - FIELDS, 256), F32)
+
+    def group(g, _):
+        planes = [[], []]
+        for k in range(4):
+            at = pl.multiple_of((g * 4 + k) * 256, 256)
+            both = cells[:, :, pl.ds(at, 256)].astype(F32)
+            for n in range(2):
+                planes[n].append(jnp.concatenate([both[:, n, :], pad], axis=0))
+        for n in range(2):
+            full = dot(jnp.concatenate(planes[n], axis=0).astype(BF16), e)
+            ghosted[n, pl.ds(2 + g * 4, 4)] = full.reshape(4, ROWS, WIDE)
+        return 0
+
+    lax.fori_loop(0, 4, group, 0)
+
+
+def build_ghosted(window, ghosted):
     lane = lax.broadcasted_iota(jnp.int32, (ROWS, WIDE), 1)
     x, y = lane // EDGE, lane % EDGE
     inside = (x >= 2) & (x < 18) & (y >= 2) & (y < 18)
-    e = spread[...]
-    pad = jnp.zeros((ROWS - FIELDS, 256), F32)
 
     def blend(n, f, parent, other):
         return 0.75 * window[n, parent] + 0.25 * window[n, other]
@@ -199,19 +212,12 @@
 
     def group(g, _):
         for n in range(2):
-            planes = []
-            for k in range(4):
-                at = pl.multiple_of((g * 4 + k) * 256, 256)
-                planes.append(jnp.concatenate([cells[n, :, pl.ds(at, 256)].astype(F32), pad], axis=0))
-            full = dot(jnp.concatenate(planes, axis=0).astype(BF16), e)
-            for k in range(4):
-                f = 2 + g * 4 + k
-                parent = 2 + g * 2 + k // 2
-                other = parent + (-1 if k % 2 == 0 else 1)
-                ghosted[n, f] = jnp.where(inside, full[k * ROWS : (k + 1) * ROWS], blend(n, f, parent, other))
+            for k in range(2):
+                f = 2 + g * 2 + k
+                ghosted[n, f] = jnp.where(inside, ghosted[n, f], blend(n, f, 2 + g, 1 + g + 2 * k))
         return 0
 
-    lax.fori_loop(0, 4, group, 0)
+    lax.fori_loop(0, 8, group, 0)
 
 
 def first_step(ghosted, z, coef, vel, gw, aw):
@@ -290,15 +296,16 @@
 
 
 def offset(c):
-    return (15 - c) // 4, lax.rem(15 - c, 4)
+    t = 15 - c
+    return lax.rem(t // 4 + t, 4), lax.rem(t, 4)
 
 
 def fused_kernel(
     corner, level, vel, owner, coarse_hbm, cells, diff_ref, grow_ref, yield_ref, spread, gather, weights,
     coarse_out, landed, order_out,
     coarse_vmem, rows, picks, window, ghosted, once, coef, grow_pad, yield_pad,
-    units, got, tiles, order, order_smem, packed, held, staged,
-    load_sem, halo_s, halo_r, tile_s, tile_r, spread_s, spread_r, deal_s, deal_r,
+    units, got, tiles, order, order_smem, packed, held, staged, relay,
+    load_sem, halo_s, halo_r, tile_s, tile_r, give_s, hold_r, stage_s, relay_s, relay_r, land_r,
 ):
     r, p = lax.axis_index("region"), lax.axis_index("patch")
     nr, np_ = lax.axis_size("region"), lax.axis_size("patch")
@@ -329,7 +336,7 @@
     loop(1, PEERS, greet)
     load = stage_coarse(coarse_hbm, coarse_vmem, load_sem)
     tiles[p] = jnp.full((8, NY), owner[0, 0], jnp.int32)
-    held[16] = jnp.zeros((UNIT, 256), BF16)
+    held[16] = jnp.zeros((2, UNIT, NY), BF16)
     gw, aw = prepare(diff_ref, vel, grow_ref, yield_ref, coef, grow_pad, yield_pad)
     load.wait()
 
@@ -352,25 +359,26 @@
         return remote(tiles.at[slot], tiles.at[slot], tile_s.at[d], tile_r.at[d], (r, lax.rem(p + d, PEERS)))
 
     loop(1, PEERS, lambda d: tile(d, p).start())
+    expand(cells, ghosted, spread)
     for copy in halos:
         copy.wait()
 
     edges = [jnp.where(hit, 0.0, 1.0) for hit in (r == 0, r == nr - 1, p == 0, p == np_ - 1)]
     fill_rows(coarse_vmem, got, rows, edges)
     build_windows(rows, corner, picks, window, weights)
-    build_ghosted(window, cells, ghosted, spread)
+    build_ghosted(window, ghosted)
     lane = lax.broadcasted_iota(jnp.int32, (ROWS, 2 * LANES), 1)
     twice = jnp.where(lane < LANES, level[0], level[1]) == 2
     for z in (1, 2, 3):
         once[z] = first_step(ghosted, z, coef, vel, gw, aw)
 
     def give(c):
-        return remote(packed.at[c], held.at[p], spread_s.at[c], spread_r.at[c], (r, peer(*offset(c))))
+        return remote(packed.at[c], held.at[p], give_s.at[c], hold_r.at[c], (r, peer(*offset(c))))
 
     def take(c):
         dy, dx = offset(c)
         source = peer(4 - dy, 4 - dx)
-        remote(packed.at[c], held.at[source], spread_s.at[c], spread_r.at[c], (r, source)).wait_recv()
+        remote(packed.at[c], held.at[source], give_s.at[c], hold_r.at[c], (r, source)).wait_recv()
 
     def plane(c):
         z = c + 2
@@ -379,7 +387,9 @@
         ahead = jnp.minimum(z + 2, 18)
         once[ahead] = first_step(ghosted, ahead, coef, vel, gw, aw)
         pair = [dot(chosen[:, n * LANES : (n + 1) * LANES], gather[...]) for n in range(2)]
-        packed[c] = pack_pair(*pair)
+        chunk = pack_pair(*pair)
+        packed[c, 0] = chunk[:, :NY]
+        packed[c, 1] = chunk[:, NY:]
 
         @pl.when(c < 15)
         def _():
@@ -409,21 +419,76 @@
     to_smem.wait()
     loop(0, 15, take)
 
-    def deal(n, dy, dx):
-        return remote(staged.at[n], landed.at[p], deal_s.at[n], deal_r.at[n], (r, peer(dy, dx)))
-
-    for n, (dy, dx) in enumerate(NEAR):
+    def send_stage(h, a, b):
+        device = peer(0, a) if h == 0 else peer(a, 0)
+        to, other, me = axes(h, a, b)
+        return remote(staged.at[h, to, other], relay.at[h, me, other], stage_s.at[h, to, other], relay_r.at[h, me, other], (r, device))
+
+    def axes(h, a, b):
+        along, across = (x, y) if h == 0 else (y, x)
+        return lax.rem(along + a, 4), lax.rem(across + b, 4), along
+
+    def wait_stage(h, a, b):
+        source, other, _ = axes(h, a, b)
+        remote(
+            staged.at[h, source, other], relay.at[h, source, other],
+            stage_s.at[h, source, other], relay_r.at[h, source, other], (r, peer(1, 1)),
+        ).wait_recv()
+
+    def send_land(h, a, b):
+        source, other, _ = axes(h, a, b)
+        src = staged.at[h, source, other] if a == 0 else relay.at[h, source, other]
+        handler = peer(0, a) if h == 0 else peer(a, 0)
+        device = peer(b, 0) if h == 0 else peer(0, b)
+        return remote(src, landed.at[handler, h], relay_s.at[h, source, other], land_r.at[h, handler], (r, device))
+
+    def wait_land(h, a, b):
+        handler = peer(b, a) if h == 0 else peer(a, b)
+        remote(
+            staged.at[h, 0, 0], landed.at[handler, h], relay_s.at[h, 0, 0], land_r.at[h, handler], (r, peer(1, 1))
+        ).wait_recv()
+
+    def stage(h, a, b):
+        to, other, _ = axes(h, a, b)
+        owner_id = peer(b, a) if h == 0 else peer(a, b)
         for k in range(2):
-            staged[n, k] = held[order_smem[0, peer(dy, dx) * 2 + k]]
-        deal(n, dy, dx).start()
-    for k in range(2):
-        landed[p, k] = held[order_smem[0, p * 2 + k]]
-    advance_coarse(rows, coarse_out, coef, vel, gw, aw, 4, 16)
+            staged[h, to, other, k] = held[order_smem[0, owner_id * 2 + k], h]
+
+    for a in (1, 3, 2):
+        for b in range(4):
+            for h in range(2):
+                stage(h, a, b)
+                send_stage(h, a, b).start()
+    for b in (0, 1, 3, 2):
+        for h in range(2):
+            stage(h, 0, b)
+            if b:
+                send_land(h, 0, b).start()
+    for h in range(2):
+        to, other, _ = axes(h, 0, 0)
+        landed[p, h] = staged[h, to, other]
+    begin = 4
+    for a in (3, 1, 2):
+        advance_coarse(rows, coarse_out, coef, vel, gw, aw, begin, begin + 4)
+        begin += 4
+        for b in (1, 3, 2, 0):
+            for h in range(2):
+                wait_stage(h, a, b)
+                if b:
+                    send_land(h, a, b).start()
+                else:
+                    source, other, _ = axes(h, a, b)
+                    landed[peer(0, a) if h == 0 else peer(a, 0), h] = relay[h, source, other]
+
     loop(0, 15, lambda c: give(c).wait_send())
-    for n, (dy, dx) in enumerate(NEAR):
-        deal(n, dy, dx).wait_send()
-        source = peer(4 - dy, 4 - dx)
-        remote(staged.at[n], landed.at[source], deal_s.at[n], deal_r.at[n], (r, source)).wait_recv()
+    for a in range(4):
+        for b in range(4):
+            for h in range(2):
+                if a:
+                    send_stage(h, a, b).wait_send()
+                if b:
+                    send_land(h, a, b).wait_send()
+                    wait_land(h, a, b)
 
 
 def fused(corner, level, vel, owner, coarse, cells, diff, grow, give):
@@ -437,7 +502,7 @@
         fused_kernel,
         out_shape=(
             jax.ShapeDtypeStruct((FIELDS * 64, NY), F32),
-            jax.ShapeDtypeStruct((PEERS, 2, UNIT, 256), BF16),
+            jax.ShapeDtypeStruct((PEERS, 2, 2, UNIT, NY), BF16),
             jax.ShapeDtypeStruct((8, NY), jnp.int32),
         ),
         in_specs=[smem] * 4 + [pl.BlockSpec(memory_space=pl.ANY)] + [vmem] * 7,
@@ -457,11 +522,14 @@
             pltpu.VMEM((PEERS, 8, NY), jnp.int32),
             pltpu.VMEM((8, NY), jnp.int32),
             pltpu.SMEM((8, NY), jnp.int32),
-            pltpu.VMEM((PLANES, UNIT, 256), BF16),
-            pltpu.VMEM((17, UNIT, 256), BF16),
-            pltpu.VMEM((15, 2, UNIT, 256), BF16),
+            pltpu.VMEM((PLANES, 2, UNIT, NY), BF16),
+            pltpu.VMEM((17, 2, UNIT, NY), BF16),
+            pltpu.VMEM((2, 4, 4, 2, UNIT, NY), BF16),
+            pltpu.VMEM((2, 4, 4, 2, UNIT, NY), BF16),
             dma,
-            dma((8,)), dma((8,)), dma((16,)), dma((16,)), dma((16,)), dma((16,)), dma((15,)), dma((15,)),
+            dma((8,)), dma((8,)), dma((16,)), dma((16,)),
+            dma((16,)), dma((16,)),
+            dma((2, 4, 4)), dma((2, 4, 4)), dma((2, 4, 4)), dma((2, 16)),
         ],
         compiler_params=pltpu.CompilerParams(
             collective_id=0, has_side_effects=True, vmem_limit_bytes=60 * 1024 * 1024
@@ -470,42 +538,63 @@
     )(corner, level, vel, owner, coarse, cells, diff, grow, give, spread, gather, weights)
 
 
-def place_kernel(order, landed, out):
+def place_kernel(order, landed, coarse, out, coarse_out, sem):
     p = lax.axis_index("patch")
     step = pl.program_id(0)
+    copy = pltpu.make_async_copy(coarse, coarse_out, sem)
+
+    @pl.when(step == 0)
+    def _():
+        copy.start()
+
     for i in range(4):
         dy, dx = offset(step * 4 + i)
-        four = []
-        for k in range(2):
-            item = jnp.minimum(order[0, p * 2 + k], PEERS - 1)
-            handler = lax.rem(item // 4 + dy, 4) * 4 + lax.rem(item + dx, 4)
-            four.extend(unpack_pair(landed[handler, k]))
-        out[:, :, pl.ds(i * 256, 256)] = jnp.stack([f[:FIELDS] for f in four], axis=1).astype(BF16)
-
-
-def place(order, landed):
+        for h in range(2):
+            four = []
+            for k in range(2):
+                item = jnp.minimum(order[0, p * 2 + k], PEERS - 1)
+                handler = lax.rem(item // 4 + dy, 4) * 4 + lax.rem(item + dx, 4)
+                four.extend(unpack_pair(landed[handler, h, k]))
+            out[:, :, pl.ds(i * 256 + h * NY, NY)] = jnp.stack([f[:FIELDS] for f in four], axis=1).astype(BF16)
+
+    @pl.when(step == 3)
+    def _():
+        copy.wait()
+
+
+def place(order, landed, coarse):
     return pl.pallas_call(
         place_kernel,
         grid=(4,),
-        out_shape=jax.ShapeDtypeStruct((FIELDS, 4, B**3), BF16),
+        out_shape=(
+            jax.ShapeDtypeStruct((FIELDS, 4, B**3), BF16),
+            jax.ShapeDtypeStruct((FIELDS * 64, NY), F32),
+        ),
         in_specs=[
             pl.BlockSpec(memory_space=pltpu.SMEM),
-            pl.BlockSpec((PEERS, 2, UNIT, 256), lambda k: (0, 0, 0, 0)),
+            pl.BlockSpec((PEERS, 2, 2, UNIT, NY), lambda k: (0, 0, 0, 0, 0)),
+            pl.BlockSpec(memory_space=pl.ANY),
         ],
-        out_specs=pl.BlockSpec((FIELDS, 4, 1024), lambda k: (0, 0, k)),
+        out_specs=(
+            pl.BlockSpec((FIELDS, 4, 1024), lambda k: (0, 0, k)),
+            pl.BlockSpec(memory_space=pl.ANY),
+        ),
+        scratch_shapes=[pltpu.SemaphoreType.DMA],
         compiler_params=pltpu.CompilerParams(vmem_limit_bytes=32 * 1024 * 1024),
         name="place",
-    )(order, landed)
+    )(order, landed, coarse)
 
 
 def shards(
     coarse, fine_patches, new_owner, corners, level_tags, diffusivity, velocity, growth_weight, yield_weight
 ):
     coarse_next, landed, order = fused(
-        corners, level_tags, velocity, new_owner, coarse.reshape(FIELDS * 64, NY), fine_patches,
+        corners, level_tags, velocity, new_owner.T, coarse.reshape(FIELDS * 64, NY),
+        jnp.transpose(fine_patches, (1, 0, 2)),
         diffusivity[None, :], growth_weight.T, yield_weight,
     )
-    fine_next = jnp.transpose(place(order, landed), (1, 0, 2))
+    fine_next, coarse_next = place(order, landed, coarse_next)
+    fine_next = jnp.transpose(fine_next, (1, 0, 2))
     return coarse_next.reshape(coarse.shape), fine_next
 
 

time: 98.9 us -> 88.6 us (0.90)
  the two profiles are of different devices: /device:TPU:112 before, /device:TPU:6 now
where the time goes in v4:
time: 88.6 us; the launch traced here: 88.3 us
  Pallas kernels  83.7 us (94%)
  local copies, waits for them, and re-layouts  3.99 us (5%)
    pallas_call x1, Pallas kernels, fused(): pl.pallas_call(fused_kernel, out_shape=(jax.ShapeDtypeStruct((FIELDS * 64...  77.9 us
    pallas_call x1, Pallas kernels, place(): pl.pallas_call(place_kernel, grid=(4,), out_shape=(jax.ShapeDtypeStruct((...  5.78 us
    unnamed x6, local copies, waits for them, and re-layouts  3.99 us

profile of v4, /device:TPU:6, one launch (start us, length us, event | category | flops | bytes accessed | tf_op | source)
XLA Modules:
  0.0 88.3 jit_solution(1806479439720331846)
XLA Ops:
  0.6 77.9 %fused.1 = (f32[4480,128]{1,0:T(8,128)}, bf16[16,2,2,144,128]{4,3,2,1,0:T(8,128)(2,1)}, s32[8,128]{1,0:T(8,128)}) custom-call(s32[2,3]{1,0:T(2,128)} %corner.1, s32[2]{0:T(128)} %level.1, f32[3]{0:T(128)} %vel.1, s32[1,2]{1,0:T(1,128)} %bitcast.10, f32[4480,128]{1,0:T(8,128)} %bitcast.7, bf16[70,2,4096]{2,1,0:T(2,128)(2,1)} %bitcast.8, f32[1,70]{1,0:T(1,128)} %bitcast.11, ...), custom_call_target="tpu_custom_call" | custom-call | tf_op jit(solution)/shard_map/fused/pallas_call | solution.py:501
  78.5 0.0 copy-start
  78.5 1.7 %copy-done = bf16[16,2,2,144,128]{4,3,2,1,0:T(8,128)(2,1)S(1)} copy-done((bf16[16,2,2,144,128]{4,3,2,1,0:T(8,128)(2,1)S(1)}, bf16[16,2,2,144,128]{4,3,2,1,0:T(8,128)(2,1)}, u32[]{:S(2)}) %copy-start) | copy-done | bytes 2359320
  80.2 0.0 copy-start.1
  80.2 1.6 %copy-done.1 = f32[4480,128]{1,0:T(8,128)S(1)} copy-done((f32[4480,128]{1,0:T(8,128)S(1)}, f32[4480,128]{1,0:T(8,128)}, u32[]{:S(2)}) %copy-start.1) | copy-done | bytes 2293784
  81.8 0.0 copy-start.2
  81.8 0.7 copy-done.2
  82.5 5.8 %place.1 = (bf16[70,4,4096]{2,1,0:T(4,128)(2,1)}, f32[4480,128]{1,0:T(8,128)}) custom-call(s32[8,128]{1,0:T(8,128)S(1)} %copy-done.2, bf16[16,2,2,144,128]{4,3,2,1,0:T(8,128)(2,1)S(1)} %copy-done, f32[4480,128]{1,0:T(8,128)S(1)} %copy-done.1), custom_call_target="tpu_custom_call" | custom-call | tf_op jit(solution)/shard_map/place/pallas_call | solution.py:566
Async XLA Ops:
  78.5 1.7 %copy-start = (bf16[16,2,2,144,128]{4,3,2,1,0:T(8,128)(2,1)S(1)}, bf16[16,2,2,144,128]{4,3,2,1,0:T(8,128)(2,1)}, u32[]{:S(2)}) copy-start(bf16[16,2,2,144,128]{4,3,2,1,0:T(8,128)(2,1)} %get-tuple-element.8.landed) | copy-start | bytes 7077892
  80.2 1.6 %copy-start.1 = (f32[4480,128]{1,0:T(8,128)S(1)}, f32[4480,128]{1,0:T(8,128)}, u32[]{:S(2)}) copy-start(f32[4480,128]{1,0:T(8,128)} %get-tuple-element.9.coarse) | copy-start | bytes 6881284
  81.8 0.7 copy-start.2

commit v5 on v4

--- a/solution.py
+++ b/solution.py
@@ -95,12 +95,19 @@
     return copy
 
 
-def fill_rows(coarse_vmem, got, rows, edges):
-    z_low, z_high, x_low, x_high = edges
-
+def fill_own(coarse_vmem, rows):
     def own(z, _):
         for x in range(8):
             rows[z + 2, :, pl.ds((x + 2) * NY, NY)] = load_rows(coarse_vmem, z, x)
+        return 0
+
+    lax.fori_loop(0, 8, own, 0)
+
+
+def fill_rows(got, rows, edges, part):
+    z_low, z_high, x_low, x_high = edges
+
+    def sides(z, _):
         a, b = unpack_pair(got[16 + z])
         rows[z + 2, :, pl.ds(0, NY)] = a * x_low
         rows[z + 2, :, pl.ds(NY, NY)] = b * x_low
@@ -109,18 +116,13 @@
         rows[z + 2, :, pl.ds(11 * NY, NY)] = b * x_high
         return 0
 
-    lax.fori_loop(0, 8, own, 0)
+    lax.fori_loop(part * 4, part * 4 + 4, sides, 0)
+    z, scale, face, corner = ((0, z_low, 0, 32), (10, z_high, 8, 36))[part]
     for x in range(WIN):
-        if x < 2:
-            low, high, side = 32 + x, 36 + x, x_low
-        elif x < 10:
-            low, high, side = x - 2, 8 + x - 2, 1.0
-        else:
-            low, high, side = 34 + x - 10, 38 + x - 10, x_high
-        for unit, z, scale in ((low, 0, z_low * side), (high, 10, z_high * side)):
-            a, b = unpack_pair(got[unit])
-            rows[z, :, pl.ds(x * NY, NY)] = a * scale
-            rows[z + 1, :, pl.ds(x * NY, NY)] = b * scale
+        unit, side = (corner + x, x_low) if x < 2 else (face + x - 2, 1.0) if x < 10 else (corner + x - 8, x_high)
+        a, b = unpack_pair(got[unit])
+        rows[z, :, pl.ds(x * NY, NY)] = a * (scale * side)
+        rows[z + 1, :, pl.ds(x * NY, NY)] = b * (scale * side)
 
 
 def advance_coarse(rows, out, coef, vel, gw, aw, first, last):
@@ -153,7 +155,7 @@
     lax.fori_loop(first, last, step, 0)
 
 
-def build_windows(rows, corner, picks, window, weights):
+def build_picks(corner, picks):
     lane = lax.broadcasted_iota(jnp.int32, (NY, 256), 1)
     row = lax.broadcasted_iota(jnp.int32, (NY, 256), 0)
     start = jnp.where(lane < NY, corner[0, 2], corner[1, 2]) - 2
@@ -162,20 +164,19 @@
         at = slot - 16 * x
         hit = jnp.logical_and(jnp.logical_and(at >= 0, at < WIN), row == start + at)
         picks[pl.ds(x * NY, NY), :] = jnp.where(hit, 1.0, 0.0).astype(BF16)
+
+
+def build_windows(rows, picks, window, weights, part):
     v = weights[...]
-
-    def group(g, _):
-        z = g * 3
-        lhs = rows[pl.ds(z, 3)].reshape(3 * ROWS, WIN * NY).astype(BF16)
-        first = dot(lhs[:, : 8 * NY], picks[...]).astype(BF16)
-        second = dot(lhs[:, 8 * NY :], picks[: 4 * NY, :]).astype(BF16)
-        for n in range(2):
-            cut = slice(n * NY, (n + 1) * NY)
-            both = jnp.concatenate([first[:, cut], second[:, cut]], axis=1)
-            window[n, pl.ds(z, 3)] = dot(both, v).reshape(3, ROWS, WIDE)
-        return 0
-
-    lax.fori_loop(0, 4, group, 0)
+    half = pl.ds(part * 6, 6)
+    low = rows[half, :, : 8 * NY].reshape(6 * ROWS, 8 * NY).astype(BF16)
+    first = dot(low, picks[...]).astype(BF16)
+    high = rows[half, :, 8 * NY :].reshape(6 * ROWS, 4 * NY).astype(BF16)
+    second = dot(high, picks[: 4 * NY, :]).astype(BF16)
+    for n in range(2):
+        cut = slice(n * NY, (n + 1) * NY)
+        both = jnp.concatenate([first[:, cut], second[:, cut]], axis=1)
+        window[n, half] = dot(both, v).reshape(6, ROWS, WIDE)
 
 
 def expand(cells, ghosted, spread):
@@ -197,27 +198,35 @@
     lax.fori_loop(0, 4, group, 0)
 
 
-def build_ghosted(window, ghosted):
+def build_ghosted(window, ghosted, part):
     lane = lax.broadcasted_iota(jnp.int32, (ROWS, WIDE), 1)
     x, y = lane // EDGE, lane % EDGE
     inside = (x >= 2) & (x < 18) & (y >= 2) & (y < 18)
 
-    def blend(n, f, parent, other):
+    def blend(n, parent, other):
         return 0.75 * window[n, parent] + 0.25 * window[n, other]
 
-    for n in range(2):
-        for f in (0, 1, 18, 19):
-            parent = f // 2 + 1
-            ghosted[n, f] = blend(n, f, parent, parent + (-1 if f % 2 == 0 else 1))
-
-    def group(g, _):
+    def frame(f, parent, other):
         for n in range(2):
-            for k in range(2):
-                f = 2 + g * 2 + k
-                ghosted[n, f] = jnp.where(inside, ghosted[n, f], blend(n, f, 2 + g, 1 + g + 2 * k))
+            ghosted[n, f] = jnp.where(inside, ghosted[n, f], blend(n, parent, other))
+
+    def pair(g, _):
+        frame(2 + g * 2, 2 + g, 1 + g)
+        frame(3 + g * 2, 2 + g, 3 + g)
         return 0
 
-    lax.fori_loop(0, 8, group, 0)
+    if part == 0:
+        for n in range(2):
+            ghosted[n, 0] = blend(n, 1, 0)
+            ghosted[n, 1] = blend(n, 1, 2)
+        lax.fori_loop(0, 3, pair, 0)
+        frame(8, 5, 4)
+    else:
+        frame(9, 5, 6)
+        lax.fori_loop(4, 8, pair, 0)
+        for n in range(2):
+            ghosted[n, 18] = blend(n, 10, 9)
+            ghosted[n, 19] = blend(n, 10, 11)
 
 
 def first_step(ghosted, z, coef, vel, gw, aw):
@@ -302,10 +311,10 @@
 
 def fused_kernel(
     corner, level, vel, owner, coarse_hbm, cells, diff_ref, grow_ref, yield_ref, spread, gather, weights,
-    coarse_out, landed, order_out,
-    coarse_vmem, rows, picks, window, ghosted, once, coef, grow_pad, yield_pad,
+    coarse_hbm_out, landed, order_out,
+    coarse_out, coarse_vmem, rows, picks, window, ghosted, once, coef, grow_pad, yield_pad,
     units, got, tiles, order, order_smem, packed, held, staged, relay,
-    load_sem, halo_s, halo_r, tile_s, tile_r, give_s, hold_r, stage_s, relay_s, relay_r, land_r,
+    load_sem, halo_s, halo_r, tile_s, tile_r, give_s, hold_r, stage_s, relay_s, relay_r, land_r, local_s, out_s,
 ):
     r, p = lax.axis_index("region"), lax.axis_index("patch")
     nr, np_ = lax.axis_size("region"), lax.axis_size("patch")
@@ -318,17 +327,19 @@
 
     halo_sends = [
         ((up_r, p), 8, 8, 0),
-        ((down_r, p), 0, 8, 8),
-        ((r, up_p), 24, 8, 16),
-        ((r, down_p), 16, 8, 24),
+        ((r, up_p), 24, 4, 16),
+        ((r, down_p), 16, 4, 24),
         ((up_r, up_p), 14, 2, 32),
         ((up_r, down_p), 8, 2, 34),
+        ((down_r, p), 0, 8, 8),
+        ((r, up_p), 28, 4, 20),
+        ((r, down_p), 20, 4, 28),
         ((down_r, up_p), 6, 2, 36),
         ((down_r, down_p), 0, 2, 38),
     ]
     barrier = pltpu.get_barrier_semaphore()
-    for device, _, _, _ in halo_sends:
-        pl.semaphore_signal(barrier, inc=1, device_id=device, device_id_type=MESH)
+    for n in (0, 1, 2, 3, 4, 5, 8, 9):
+        pl.semaphore_signal(barrier, inc=1, device_id=halo_sends[n][0], device_id_type=MESH)
 
     def greet(d):
         pl.semaphore_signal(barrier, inc=1, device_id=(r, lax.rem(p + d, PEERS)), device_id_type=MESH)
@@ -359,14 +370,20 @@
         return remote(tiles.at[slot], tiles.at[slot], tile_s.at[d], tile_r.at[d], (r, lax.rem(p + d, PEERS)))
 
     loop(1, PEERS, lambda d: tile(d, p).start())
+    fill_own(coarse_vmem, rows)
+    build_picks(corner, picks)
     expand(cells, ghosted, spread)
-    for copy in halos:
+    for copy in halos[:5]:
         copy.wait()
 
     edges = [jnp.where(hit, 0.0, 1.0) for hit in (r == 0, r == nr - 1, p == 0, p == np_ - 1)]
-    fill_rows(coarse_vmem, got, rows, edges)
-    build_windows(rows, corner, picks, window, weights)
-    build_ghosted(window, ghosted)
+
+    def frames(part):
+        fill_rows(got, rows, edges, part)
+        build_windows(rows, picks, window, weights, part)
+        build_ghosted(window, ghosted, part)
+
+    frames(0)
     lane = lax.broadcasted_iota(jnp.int32, (ROWS, 2 * LANES), 1)
     twice = jnp.where(lane < LANES, level[0], level[1]) == 2
     for z in (1, 2, 3):
@@ -395,7 +412,11 @@
         def _():
             give(c).start()
 
-    loop(0, PLANES, plane)
+    loop(0, 4, plane)
+    for copy in halos[5:]:
+        copy.wait()
+    frames(1)
+    loop(4, PLANES, plane)
     held[p] = packed[15]
     advance_coarse(rows, coarse_out, coef, vel, gw, aw, 0, 4)
 
@@ -413,7 +434,8 @@
             slot = slot + jnp.where(owners[j] == owners[i], 1, 0)
         pick = jnp.where(slot == lane, i, pick)
     order[...] = pick
-    order_out[...] = pick
+    keep_order = pltpu.make_async_copy(order, order_out, out_s.at[0])
+    keep_order.start()
     to_smem = pltpu.make_async_copy(order, order_smem, load_sem)
     to_smem.start()
     to_smem.wait()
@@ -447,6 +469,9 @@
         remote(
             staged.at[h, 0, 0], landed.at[handler, h], relay_s.at[h, 0, 0], land_r.at[h, handler], (r, peer(1, 1))
         ).wait_recv()
+
+    def here(h, a, src, handler):
+        return pltpu.make_async_copy(src, landed.at[handler, h], local_s.at[h, a])
 
     def stage(h, a, b):
         to, other, _ = axes(h, a, b)
@@ -466,7 +491,7 @@
                 send_land(h, 0, b).start()
     for h in range(2):
         to, other, _ = axes(h, 0, 0)
-        landed[p, h] = staged[h, to, other]
+        here(h, 0, staged.at[h, to, other], p).start()
     begin = 4
     for a in (3, 1, 2):
         advance_coarse(rows, coarse_out, coef, vel, gw, aw, begin, begin + 4)
@@ -478,8 +503,10 @@
                     send_land(h, a, b).start()
                 else:
                     source, other, _ = axes(h, a, b)
-                    landed[peer(0, a) if h == 0 else peer(a, 0), h] = relay[h, source, other]
-
+                    here(h, a, relay.at[h, source, other], peer(0, a) if h == 0 else peer(a, 0)).start()
+
+    keep_coarse = pltpu.make_async_copy(coarse_out, coarse_hbm_out, out_s.at[1])
+    keep_coarse.start()
     loop(0, 15, lambda c: give(c).wait_send())
     for a in range(4):
         for b in range(4):
@@ -489,6 +516,11 @@
                 if b:
                     send_land(h, a, b).wait_send()
                     wait_land(h, a, b)
+    for h in range(2):
+        for a in range(4):
+            here(h, a, staged.at[h, 0, 0], p).wait()
+    keep_order.wait()
+    keep_coarse.wait()
 
 
 def fused(corner, level, vel, owner, coarse, cells, diff, grow, give):
@@ -506,8 +538,9 @@
             jax.ShapeDtypeStruct((8, NY), jnp.int32),
         ),
         in_specs=[smem] * 4 + [pl.BlockSpec(memory_space=pl.ANY)] + [vmem] * 7,
-        out_specs=(vmem, vmem, vmem),
+        out_specs=(pl.BlockSpec(memory_space=pltpu.HBM),) * 3,
         scratch_shapes=[
+            pltpu.VMEM((FIELDS * 64, NY), F32),
             pltpu.VMEM((ROWS * 64, NY), F32),
             pltpu.VMEM((WIN, ROWS, WIN * NY), F32),
             pltpu.VMEM((8 * NY, 256), BF16),
@@ -527,9 +560,9 @@
             pltpu.VMEM((2, 4, 4, 2, UNIT, NY), BF16),
             pltpu.VMEM((2, 4, 4, 2, UNIT, NY), BF16),
             dma,
-            dma((8,)), dma((8,)), dma((16,)), dma((16,)),
+            dma((10,)), dma((10,)), dma((16,)), dma((16,)),
             dma((16,)), dma((16,)),
-            dma((2, 4, 4)), dma((2, 4, 4)), dma((2, 4, 4)), dma((2, 16)),
+            dma((2, 4, 4)), dma((2, 4, 4)), dma((2, 4, 4)), dma((2, 16)), dma((2, 4)), dma((2,)),
         ],
         compiler_params=pltpu.CompilerParams(
             collective_id=0, has_side_effects=True, vmem_limit_bytes=60 * 1024 * 1024
@@ -538,49 +571,63 @@
     )(corner, level, vel, owner, coarse, cells, diff, grow, give, spread, gather, weights)
 
 
-def place_kernel(order, landed, coarse, out, coarse_out, sem):
+def place_kernel(order, landed, coarse, out, coarse_out, chunks, block, load_sem, sem):
     p = lax.axis_index("patch")
     step = pl.program_id(0)
-    copy = pltpu.make_async_copy(coarse, coarse_out, sem)
+    fetch = pltpu.make_async_copy(coarse, block, sem.at[0])
+    keep = pltpu.make_async_copy(block, coarse_out, sem.at[1])
+
+    def load(c, k):
+        dy, dx = offset(c)
+        item = jnp.minimum(order[0, p * 2 + k], PEERS - 1)
+        handler = lax.rem(item // 4 + dy, 4) * 4 + lax.rem(item + dx, 4)
+        return pltpu.make_async_copy(landed.at[handler, :, k], chunks.at[c, k], load_sem.at[c, k])
 
     @pl.when(step == 0)
     def _():
-        copy.start()
-
-    for i in range(4):
-        dy, dx = offset(step * 4 + i)
+        def start(c):
+            for k in range(2):
+                load(c, k).start()
+
+        loop(0, PLANES, start)
+        fetch.start()
+
+    for i in range(2):
+        c = step * 2 + i
+        for k in range(2):
+            load(c, k).wait()
         for h in range(2):
-            four = []
-            for k in range(2):
-                item = jnp.minimum(order[0, p * 2 + k], PEERS - 1)
-                handler = lax.rem(item // 4 + dy, 4) * 4 + lax.rem(item + dx, 4)
-                four.extend(unpack_pair(landed[handler, h, k]))
+            four = [f for k in range(2) for f in unpack_pair(chunks[c, k, h])]
             out[:, :, pl.ds(i * 256 + h * NY, NY)] = jnp.stack([f[:FIELDS] for f in four], axis=1).astype(BF16)
 
     @pl.when(step == 3)
     def _():
-        copy.wait()
+        fetch.wait()
+        keep.start()
+
+    @pl.when(step == 7)
+    def _():
+        keep.wait()
 
 
 def place(order, landed, coarse):
+    hbm = pl.BlockSpec(memory_space=pltpu.HBM)
     return pl.pallas_call(
         place_kernel,
-        grid=(4,),
+        grid=(8,),
         out_shape=(
             jax.ShapeDtypeStruct((FIELDS, 4, B**3), BF16),
             jax.ShapeDtypeStruct((FIELDS * 64, NY), F32),
         ),
-        in_specs=[
-            pl.BlockSpec(memory_space=pltpu.SMEM),
-            pl.BlockSpec((PEERS, 2, 2, UNIT, NY), lambda k: (0, 0, 0, 0, 0)),
-            pl.BlockSpec(memory_space=pl.ANY),
+        in_specs=[pl.BlockSpec(memory_space=pltpu.SMEM), hbm, hbm],
+        out_specs=(pl.BlockSpec((FIELDS, 4, 512), lambda k: (0, 0, k)), hbm),
+        scratch_shapes=[
+            pltpu.VMEM((PLANES, 2, 2, UNIT, NY), BF16),
+            pltpu.VMEM((FIELDS * 64, NY), F32),
+            pltpu.SemaphoreType.DMA((PLANES, 2)),
+            pltpu.SemaphoreType.DMA((2,)),
         ],
-        out_specs=(
-            pl.BlockSpec((FIELDS, 4, 1024), lambda k: (0, 0, k)),
-            pl.BlockSpec(memory_space=pl.ANY),
-        ),
-        scratch_shapes=[pltpu.SemaphoreType.DMA],
-        compiler_params=pltpu.CompilerParams(vmem_limit_bytes=32 * 1024 * 1024),
+        compiler_params=pltpu.CompilerParams(vmem_limit_bytes=60 * 1024 * 1024),
         name="place",
     )(order, landed, coarse)
 

time: 88.6 us -> 79.3 us (0.90)
  Pallas kernels: 83.7 us -> 78.4 us
  local copies, waits for them, and re-layouts: 3.99 us -> 0 us
    pallas_call x1, Pallas kernels: 77.9 us -> 70.1 us  [fused(): pl.pallas_call(fused_kernel, out_shape=(jax.ShapeDtypeStruct((FIELDS * 64...]
    unnamed x6 -> x0, local copies, waits for them, and re-layouts: 3.99 us -> none
    pallas_call x1, Pallas kernels: 5.78 us -> 8.36 us  [place(): pl.pallas_call(place_kernel, grid=(8,), out_shape=(jax.ShapeDtypeStruct((...]
where the time goes in v5:
time: 79.3 us; the launch traced here: 79.1 us
  Pallas kernels  78.4 us (99%)
    pallas_call x1, Pallas kernels, fused(): pl.pallas_call(fused_kernel, out_shape=(jax.ShapeDtypeStruct((FIELDS * 64...  70.1 us
    pallas_call x1, Pallas kernels, place(): pl.pallas_call(place_kernel, grid=(8,), out_shape=(jax.ShapeDtypeStruct((...  8.36 us

profile of v5, /device:TPU:6, one launch (start us, length us, event | category | flops | bytes accessed | tf_op | source)
XLA Modules:
  0.0 79.1 jit_solution(2665936920353783323)
XLA Ops:
  0.6 70.1 %fused.1 = (f32[4480,128]{1,0:T(8,128)}, bf16[16,2,2,144,128]{4,3,2,1,0:T(8,128)(2,1)}, s32[8,128]{1,0:T(8,128)}) custom-call(s32[2,3]{1,0:T(2,128)} %corner.1, s32[2]{0:T(128)} %level.1, f32[3]{0:T(128)} %vel.1, s32[1,2]{1,0:T(1,128)} %bitcast.10, f32[4480,128]{1,0:T(8,128)} %bitcast.7, bf16[70,2,4096]{2,1,0:T(2,128)(2,1)} %bitcast.8, f32[1,70]{1,0:T(1,128)} %bitcast.11, ...), custom_call_target="tpu_custom_call" | custom-call | tf_op jit(solution)/shard_map/fused/pallas_call | solution.py:533
  70.7 8.4 %place.1 = (bf16[70,4,4096]{2,1,0:T(4,128)(2,1)}, f32[4480,128]{1,0:T(8,128)}) custom-call(s32[8,128]{1,0:T(8,128)} %get-tuple-element.7.order, bf16[16,2,2,144,128]{4,3,2,1,0:T(8,128)(2,1)} %get-tuple-element.8.landed, f32[4480,128]{1,0:T(8,128)} %get-tuple-element.9.coarse), custom_call_target="tpu_custom_call" | custom-call | tf_op jit(solution)/shard_map/place/pallas_call | solution.py:615

commit v6 on v5

--- a/solution.py
+++ b/solution.py
@@ -20,6 +20,7 @@
 NY = 128
 PLANES = 16
 PEERS = 16
+COLUMN = 6
 UNIT = 144
 MESH = pl.DeviceIdType.MESH
 F32 = jnp.float32
@@ -313,7 +314,7 @@
     corner, level, vel, owner, coarse_hbm, cells, diff_ref, grow_ref, yield_ref, spread, gather, weights,
     coarse_hbm_out, landed, order_out,
     coarse_out, coarse_vmem, rows, picks, window, ghosted, once, coef, grow_pad, yield_pad,
-    units, got, tiles, order, order_smem, packed, held, staged, relay,
+    units, got, tiles, order, order_smem, packed, held, staged, fwd, relay01, relay02, relay03, relay11, relay12, relay13,
     load_sem, halo_s, halo_r, tile_s, tile_r, give_s, hold_r, stage_s, relay_s, relay_r, land_r, local_s, out_s,
 ):
     r, p = lax.axis_index("region"), lax.axis_index("patch")
@@ -348,6 +349,10 @@
     load = stage_coarse(coarse_hbm, coarse_vmem, load_sem)
     tiles[p] = jnp.full((8, NY), owner[0, 0], jnp.int32)
     held[16] = jnp.zeros((2, UNIT, NY), BF16)
+    relay = ((None, relay01, relay02, relay03), (None, relay11, relay12, relay13))
+    for h in range(2):
+        for a in (1, 2, 3):
+            relay[h][a][COLUMN] = jnp.zeros((UNIT, NY), BF16)
     gw, aw = prepare(diff_ref, vel, grow_ref, yield_ref, coef, grow_pad, yield_pad)
     load.wait()
 
@@ -426,14 +431,38 @@
 
     loop(1, PEERS, settle)
     lane = lax.broadcasted_iota(jnp.int32, (8, NY), 1)
+    row = lax.broadcasted_iota(jnp.int32, (8, NY), 0)
     owners = [tiles[i] for i in range(PEERS)]
+
+    def one(hit):
+        return jnp.where(hit, 1, 0)
+
+    here_y, here_x = lane // 8, lax.rem(lane // 2, 4)
     pick = jnp.full((8, NY), 16, jnp.int32)
+    pick_x, pick_y = pick, pick
+    ahead_x = lax.rem(lane, 2)
+    ahead_y = ahead_x
     for i in range(PEERS):
-        slot = owners[i] * 2
-        for j in range(i):
-            slot = slot + jnp.where(owners[j] == owners[i], 1, 0)
-        pick = jnp.where(slot == lane, i, pick)
-    order[...] = pick
+        oy, ox = owners[i] // 4, lax.rem(owners[i], 4)
+        rank = jnp.zeros((8, NY), jnp.int32)
+        before_x, before_y = rank, rank
+        for j in range(PEERS):
+            jy, jx = owners[j] // 4, lax.rem(owners[j], 4)
+            if j < i:
+                rank = rank + one(owners[j] == owners[i])
+            before_x = before_x + one((jx == ox) & (jy < oy))
+            before_y = before_y + one((jy == oy) & (jx < ox))
+        pick = jnp.where(owners[i] * 2 + rank == lane, i, pick)
+        pick_x = jnp.where(ox * 8 + before_x + rank == lane, i, pick_x)
+        pick_y = jnp.where(oy * 8 + before_y + rank == lane, i, pick_y)
+        ahead_x = ahead_x + one((ox == here_x) & (oy < here_y))
+        ahead_y = ahead_y + one((oy == here_y) & (ox < here_x))
+    ahead_x = jnp.where(pick < 16, jnp.minimum(ahead_x, COLUMN), COLUMN)
+    ahead_y = jnp.where(pick < 16, jnp.minimum(ahead_y, COLUMN), COLUMN)
+    table = pick
+    for n, part in enumerate((pick_x, pick_y, ahead_x, ahead_y)):
+        table = jnp.where(row == n + 1, part, table)
+    order[...] = table
     keep_order = pltpu.make_async_copy(order, order_out, out_s.at[0])
     keep_order.start()
     to_smem = pltpu.make_async_copy(order, order_smem, load_sem)
@@ -441,84 +470,68 @@
     to_smem.wait()
     loop(0, 15, take)
 
-    def send_stage(h, a, b):
-        device = peer(0, a) if h == 0 else peer(a, 0)
-        to, other, me = axes(h, a, b)
-        return remote(staged.at[h, to, other], relay.at[h, me, other], stage_s.at[h, to, other], relay_r.at[h, me, other], (r, device))
-
-    def axes(h, a, b):
-        along, across = (x, y) if h == 0 else (y, x)
-        return lax.rem(along + a, 4), lax.rem(across + b, 4), along
-
-    def wait_stage(h, a, b):
-        source, other, _ = axes(h, a, b)
+    def along(h, a):
+        return peer(0, a) if h == 0 else peer(a, 0)
+
+    def across(h, b):
+        return peer(b, 0) if h == 0 else peer(0, b)
+
+    def send_stage(h, a):
+        return remote(
+            staged.at[h, a], relay[h][4 - a].at[pl.ds(0, COLUMN)], stage_s.at[h, a], relay_r.at[h, 4 - a], (r, along(h, a))
+        )
+
+    def wait_stage(h, a):
         remote(
-            staged.at[h, source, other], relay.at[h, source, other],
-            stage_s.at[h, source, other], relay_r.at[h, source, other], (r, peer(1, 1)),
+            staged.at[h, a], relay[h][a].at[pl.ds(0, COLUMN)], stage_s.at[h, a], relay_r.at[h, a], (r, along(h, a))
         ).wait_recv()
 
     def send_land(h, a, b):
-        source, other, _ = axes(h, a, b)
-        src = staged.at[h, source, other] if a == 0 else relay.at[h, source, other]
-        handler = peer(0, a) if h == 0 else peer(a, 0)
-        device = peer(b, 0) if h == 0 else peer(0, b)
-        return remote(src, landed.at[handler, h], relay_s.at[h, source, other], land_r.at[h, handler], (r, device))
+        handler = along(h, a)
+        return remote(fwd.at[h, a, b], landed.at[handler, h], relay_s.at[h, a, b], land_r.at[h, handler], (r, across(h, b)))
 
     def wait_land(h, a, b):
         handler = peer(b, a) if h == 0 else peer(a, b)
-        remote(
-            staged.at[h, 0, 0], landed.at[handler, h], relay_s.at[h, 0, 0], land_r.at[h, handler], (r, peer(1, 1))
-        ).wait_recv()
-
-    def here(h, a, src, handler):
-        return pltpu.make_async_copy(src, landed.at[handler, h], local_s.at[h, a])
-
-    def stage(h, a, b):
-        to, other, _ = axes(h, a, b)
-        owner_id = peer(b, a) if h == 0 else peer(a, b)
-        for k in range(2):
-            staged[h, to, other, k] = held[order_smem[0, owner_id * 2 + k], h]
+        remote(fwd.at[h, a, b], landed.at[handler, h], relay_s.at[h, a, b], land_r.at[h, handler], (r, across(h, b))).wait_recv()
+
+    def here(h, a):
+        return pltpu.make_async_copy(fwd.at[h, a, 0], landed.at[along(h, a), h], local_s.at[h, a])
 
     for a in (1, 3, 2):
-        for b in range(4):
-            for h in range(2):
-                stage(h, a, b)
-                send_stage(h, a, b).start()
-    for b in (0, 1, 3, 2):
         for h in range(2):
-            stage(h, 0, b)
-            if b:
-                send_land(h, 0, b).start()
-    for h in range(2):
-        to, other, _ = axes(h, 0, 0)
-        here(h, 0, staged.at[h, to, other], p).start()
-    begin = 4
-    for a in (3, 1, 2):
-        advance_coarse(rows, coarse_out, coef, vel, gw, aw, begin, begin + 4)
-        begin += 4
-        for b in (1, 3, 2, 0):
-            for h in range(2):
-                wait_stage(h, a, b)
+            group = lax.rem((x if h == 0 else y) + a, 4)
+            for m in range(COLUMN):
+                staged[h, a, m] = held[order_smem[1 + h, group * 8 + m], h]
+            send_stage(h, a).start()
+    for a in (0, 3, 1, 2):
+        if a:
+            begin = {3: 4, 1: 8, 2: 12}[a]
+            advance_coarse(rows, coarse_out, coef, vel, gw, aw, begin, begin + 4)
+        for h in range(2):
+            if a:
+                wait_stage(h, a)
+            for b in (1, 3, 2, 0):
+                owner_id = across(h, b)
+                for k in range(2):
+                    if a:
+                        fwd[h, a, b, k] = relay[h][a][jnp.clip(order_smem[3 + h, owner_id * 2 + k], 0, COLUMN)]
+                    else:
+                        fwd[h, a, b, k] = held[order_smem[0, owner_id * 2 + k], h]
                 if b:
                     send_land(h, a, b).start()
                 else:
-                    source, other, _ = axes(h, a, b)
-                    here(h, a, relay.at[h, source, other], peer(0, a) if h == 0 else peer(a, 0)).start()
-
+                    here(h, a).start()
     keep_coarse = pltpu.make_async_copy(coarse_out, coarse_hbm_out, out_s.at[1])
     keep_coarse.start()
     loop(0, 15, lambda c: give(c).wait_send())
-    for a in range(4):
-        for b in range(4):
-            for h in range(2):
-                if a:
-                    send_stage(h, a, b).wait_send()
-                if b:
-                    send_land(h, a, b).wait_send()
-                    wait_land(h, a, b)
     for h in range(2):
         for a in range(4):
-            here(h, a, staged.at[h, 0, 0], p).wait()
+            if a:
+                send_stage(h, a).wait_send()
+            here(h, a).wait()
+            for b in (1, 2, 3):
+                send_land(h, a, b).wait_send()
+                wait_land(h, a, b)
     keep_order.wait()
     keep_coarse.wait()
 
@@ -557,12 +570,15 @@
             pltpu.SMEM((8, NY), jnp.int32),
             pltpu.VMEM((PLANES, 2, UNIT, NY), BF16),
             pltpu.VMEM((17, 2, UNIT, NY), BF16),
+            pltpu.VMEM((2, 4, COLUMN, UNIT, NY), BF16),
             pltpu.VMEM((2, 4, 4, 2, UNIT, NY), BF16),
-            pltpu.VMEM((2, 4, 4, 2, UNIT, NY), BF16),
+        ]
+        + [pltpu.VMEM((COLUMN + 1, UNIT, NY), BF16)] * 6
+        + [
             dma,
             dma((10,)), dma((10,)), dma((16,)), dma((16,)),
             dma((16,)), dma((16,)),
-            dma((2, 4, 4)), dma((2, 4, 4)), dma((2, 4, 4)), dma((2, 16)), dma((2, 4)), dma((2,)),
+            dma((2, 4)), dma((2, 4, 4)), dma((2, 4)), dma((2, 16)), dma((2, 4)), dma((2,)),
         ],
         compiler_params=pltpu.CompilerParams(
             collective_id=0, has_side_effects=True, vmem_limit_bytes=60 * 1024 * 1024

time: 79.3 us -> 75.6 us (0.953)
  Pallas kernels: 78.4 us -> 74.7 us
    pallas_call x1, Pallas kernels: 70.1 us -> 66.4 us  [fused(): pl.pallas_call(fused_kernel, out_shape=(jax.ShapeDtypeStruct((FIELDS * 64...]
where the time goes in v6:
time: 75.6 us; the launch traced here: 75.4 us
  Pallas kernels  74.7 us (99%)
    pallas_call x1, Pallas kernels, fused(): pl.pallas_call(fused_kernel, out_shape=(jax.ShapeDtypeStruct((FIELDS * 64...  66.4 us
    pallas_call x1, Pallas kernels, place(): pl.pallas_call(place_kernel, grid=(8,), out_shape=(jax.ShapeDtypeStruct((...  8.36 us

profile of v6, /device:TPU:6, one launch (start us, length us, event | category | flops | bytes accessed | tf_op | source)
XLA Modules:
  0.0 75.4 jit_solution(7271497356771497627)
XLA Ops:
  0.6 66.4 %fused.1 = (f32[4480,128]{1,0:T(8,128)}, bf16[16,2,2,144,128]{4,3,2,1,0:T(8,128)(2,1)}, s32[8,128]{1,0:T(8,128)}) custom-call(s32[2,3]{1,0:T(2,128)} %corner.1, s32[2]{0:T(128)} %level.1, f32[3]{0:T(128)} %vel.1, s32[1,2]{1,0:T(1,128)} %bitcast.10, f32[4480,128]{1,0:T(8,128)} %bitcast.7, bf16[70,2,4096]{2,1,0:T(2,128)(2,1)} %bitcast.8, f32[1,70]{1,0:T(1,128)} %bitcast.11, ...), custom_call_target="tpu_custom_call" | custom-call | tf_op jit(solution)/shard_map/fused/pallas_call | solution.py:546
  67.0 8.4 %place.1 = (bf16[70,4,4096]{2,1,0:T(4,128)(2,1)}, f32[4480,128]{1,0:T(8,128)}) custom-call(s32[8,128]{1,0:T(8,128)} %get-tuple-element.7.order, bf16[16,2,2,144,128]{4,3,2,1,0:T(8,128)(2,1)} %get-tuple-element.8.landed, f32[4480,128]{1,0:T(8,128)} %get-tuple-element.9.coarse), custom_call_target="tpu_custom_call" | custom-call | tf_op jit(solution)/shard_map/place/pallas_call | solution.py:631

commit v7 on v6

--- a/solution.py
+++ b/solution.py
@@ -608,20 +608,20 @@
         loop(0, PLANES, start)
         fetch.start()
 
-    for i in range(2):
-        c = step * 2 + i
+    for i in range(4):
+        c = step * 4 + i
         for k in range(2):
             load(c, k).wait()
         for h in range(2):
             four = [f for k in range(2) for f in unpack_pair(chunks[c, k, h])]
             out[:, :, pl.ds(i * 256 + h * NY, NY)] = jnp.stack([f[:FIELDS] for f in four], axis=1).astype(BF16)
 
-    @pl.when(step == 3)
+    @pl.when(step == 1)
     def _():
         fetch.wait()
         keep.start()
 
-    @pl.when(step == 7)
+    @pl.when(step == 3)
     def _():
         keep.wait()
 
@@ -630,13 +630,13 @@
     hbm = pl.BlockSpec(memory_space=pltpu.HBM)
     return pl.pallas_call(
         place_kernel,
-        grid=(8,),
+        grid=(4,),
         out_shape=(
             jax.ShapeDtypeStruct((FIELDS, 4, B**3), BF16),
             jax.ShapeDtypeStruct((FIELDS * 64, NY), F32),
         ),
         in_specs=[pl.BlockSpec(memory_space=pltpu.SMEM), hbm, hbm],
-        out_specs=(pl.BlockSpec((FIELDS, 4, 512), lambda k: (0, 0, k)), hbm),
+        out_specs=(pl.BlockSpec((FIELDS, 4, 1024), lambda k: (0, 0, k)), hbm),
         scratch_shapes=[
             pltpu.VMEM((PLANES, 2, 2, UNIT, NY), BF16),
             pltpu.VMEM((FIELDS * 64, NY), F32),

time: 75.6 us -> 74.9 us (level)
  no operation moved by 1% of the time
where the time goes in v7:
time: 74.9 us; the launch traced here: 74.7 us
  Pallas kernels  74 us (99%)
    pallas_call x1, Pallas kernels, fused(): pl.pallas_call(fused_kernel, out_shape=(jax.ShapeDtypeStruct((FIELDS * 64...  66.4 us
    pallas_call x1, Pallas kernels, place(): pl.pallas_call(place_kernel, grid=(4,), out_shape=(jax.ShapeDtypeStruct((...  7.64 us

profile of v7, /device:TPU:6, one launch (start us, length us, event | category | flops | bytes accessed | tf_op | source)
XLA Modules:
  0.0 74.7 jit_solution(12551768938984234260)
XLA Ops:
  0.6 66.4 %fused.1 = (f32[4480,128]{1,0:T(8,128)}, bf16[16,2,2,144,128]{4,3,2,1,0:T(8,128)(2,1)}, s32[8,128]{1,0:T(8,128)}) custom-call(s32[2,3]{1,0:T(2,128)} %corner.1, s32[2]{0:T(128)} %level.1, f32[3]{0:T(128)} %vel.1, s32[1,2]{1,0:T(1,128)} %bitcast.10, f32[4480,128]{1,0:T(8,128)} %bitcast.7, bf16[70,2,4096]{2,1,0:T(2,128)(2,1)} %bitcast.8, f32[1,70]{1,0:T(1,128)} %bitcast.11, ...), custom_call_target="tpu_custom_call" | custom-call | tf_op jit(solution)/shard_map/fused/pallas_call | solution.py:546
  67.0 7.6 %place.1 = (bf16[70,4,4096]{2,1,0:T(4,128)(2,1)}, f32[4480,128]{1,0:T(8,128)}) custom-call(s32[8,128]{1,0:T(8,128)} %get-tuple-element.7.order, bf16[16,2,2,144,128]{4,3,2,1,0:T(8,128)(2,1)} %get-tuple-element.8.landed, f32[4480,128]{1,0:T(8,128)} %get-tuple-element.9.coarse), custom_call_target="tpu_custom_call" | custom-call | tf_op jit(solution)/shard_map/place/pallas_call | solution.py:631
